TPU v7x, 128 devices: a whole 4x4x4 slice. The times are simulated.
128 devices in a mesh: users: 32 (over x_hi, y, z), items: 4 (over x_lo, core).
Axes of the slice: x: 4 (x_hi: 2, x_lo: 2; x = x_hi * 2 + x_lo), y: 4, z: 4, core: 2. Of those that a mesh axis runs over, the one named last changes fastest.
Arguments:
- tile_rows: int32 [32, 4, 512], P('users', 'items'), may hold values from 0 to 63, as said below
- tile_cols: int32 [32, 4, 512], P('users', 'items'), may hold values from 0 to 63, as said below
- tile_count: int32 [32, 4], P('users', 'items'), may hold values from 64 to 512, as said below
- tile_vals: bfloat16 [32, 4, 512, 128, 128], P('users', 'items'), may hold values from -6 to 6
- user_degree: int32 [262144], P(('users', 'items')), may hold values from 16 to 575
- item_degree: int32 [32768], P(('items', 'users')), may hold values from 16 to 575
- start_items: bfloat16 [64, 32768], P(None, ('items', 'users')), may hold values from -6 to 6
Outputs:
- user_panel: float32 [64, 262144], P(None, ('users', 'items'))
- item_panel: float32 [64, 32768], P(None, ('items', 'users'))
Inputs may be any that keep to these rules, and one draw needn't show every extreme that they name: Within one user block and item block, the pairs (tile_rows, tile_cols) of all 512 slots are distinct. `tile_cols`: paired with tile_rows slot by slot. Only the first tile_count slots of a block are live; some block is full in every draw.
All inputs are finite; a program needn't handle non-finite values.
Results may differ from a plain program's by a relative error of at most 0.0003.
Values sent between devices are 32-bit elements; how exact they have to be, the bound alone decides.
A program may use at most 128 MiB of HBM per device.

v0:
```python
import jax
import jax.numpy as jnp
from jax import lax
from jax.sharding import PartitionSpec as P

K = 64
TILE = 128
ITERS = 2
UT = 64
IT = 64


def local_gram(raw):
    return jnp.einsum(
        "kr,jr->kj", raw, raw, precision=lax.Precision.HIGHEST, preferred_element_type=jnp.float32
    )


def solve_panel(gram, raw):
    lower = jnp.linalg.cholesky(gram)
    return lax.linalg.triangular_solve(lower, raw, left_side=True, lower=True)


def user_partial(full_items, rows, cols, values, live_weight):
    picked = jnp.take(full_items.reshape(K, IT, TILE), cols, axis=1)
    product = jnp.einsum(
        "ktc,trc->ktr",
        picked,
        values,
        precision=lax.Precision.HIGHEST,
        preferred_element_type=jnp.float32,
    )
    product = product * live_weight[None, :, None]
    summed = jnp.zeros((K, UT, TILE), jnp.float32).at[:, rows, :].add(product)
    return summed.reshape(K, UT * TILE)


def item_partial(full_users, rows, cols, values, live_weight):
    picked = jnp.take(full_users.reshape(K, UT, TILE), rows, axis=1)
    product = jnp.einsum(
        "ktr,trc->ktc",
        picked,
        values,
        precision=lax.Precision.HIGHEST,
        preferred_element_type=jnp.float32,
    )
    product = product * live_weight[None, :, None]
    summed = jnp.zeros((K, IT, TILE), jnp.float32).at[:, cols, :].add(product)
    return summed.reshape(K, IT * TILE)


def gather_items(sent):
    return lax.all_gather(sent, "users", axis=1, tiled=True)


def body(tile_rows, tile_cols, tile_count, tile_vals, user_degree, item_degree, start_items):
    rows = tile_rows[0, 0]
    cols = tile_cols[0, 0]
    values = tile_vals[0, 0].astype(jnp.float32)
    slots = values.shape[0]
    live_weight = (jnp.arange(slots, dtype=jnp.int32) < tile_count[0, 0]).astype(jnp.float32)
    user_scale = lax.rsqrt(user_degree.astype(jnp.float32))
    item_scale = lax.rsqrt(item_degree.astype(jnp.float32))
    user_groups = lax.axis_size("users")
    item_groups = lax.axis_size("items")
    user_total = UT * TILE * user_groups
    item_total = IT * TILE * item_groups
    user_width = UT * TILE // item_groups
    panel = start_items.astype(jnp.float32)
    user_panel = jnp.zeros((K, user_width), jnp.float32)
    for step in range(ITERS):
        full_items = gather_items(item_scale[None, :] * panel)
        partial_users = user_partial(full_items, rows, cols, values, live_weight)
        user_raw = user_scale[None, :] * lax.psum_scatter(
            partial_users, "items", scatter_dimension=1, tiled=True
        )
        user_gram = lax.psum(local_gram(user_raw), ("users", "items"))
        user_panel = solve_panel(user_gram / user_total, user_raw)
        full_users = lax.all_gather(user_scale[None, :] * user_panel, "items", axis=1, tiled=True)
        partial_items = item_partial(full_users, rows, cols, values, live_weight)
        item_raw = item_scale[None, :] * lax.psum_scatter(
            partial_items, "users", scatter_dimension=1, tiled=True
        )
        item_gram = lax.psum(local_gram(item_raw), ("users", "items"))
        panel = solve_panel(item_gram / item_total, item_raw)
    return (user_panel, panel)


def solution(mesh):
    in_specs = (
        P("users", "items", None),
        P("users", "items", None),
        P("users", "items"),
        P("users", "items", None, None, None),
        P(("users", "items")),
        P(("items", "users")),
        P(None, ("items", "users")),
    )
    out_specs = (P(None, ("users", "items")), P(None, ("items", "users")))
    return jax.shard_map(body, mesh=mesh, in_specs=in_specs, out_specs=out_specs, check_vma=False)
```

profile of v0, /device:TPU:1, one launch (start us, length us, event | category | flops | bytes accessed | tf_op | source)
XLA Modules:
  0.0 1334.2 jit_solution(16207295997053255421)
XLA Ops:
  12.1 72.5 %all-gather.5.cloned.1.call-done = f32[64,8192]{1,0:T(8,128)} async-done(((f32[64,256]{1,0:T(8,128)}), f32[64,8192]{1,0:T(8,128)}) %all-gather.5.cloned.1.call-update) | async-done | bytes 2097168 | tf_op jit(solution)/shard_map/all_gather | solution.py:53
  86.4 7.0 gather_fusion
  93.4 37.3 %broadcast_multiply_fusion.3 = f32[512,64,128]{2,1,0:T(8,128)} fusion(f32[512]{0:T(512)S(1)} %get-tuple-element.8, bf16[1,1,512,128,128]{4,3,2,1,0:T(8,128)(2,1)} %param.17, f32[512,64,128]{2,1,0:T(8,128)} %gather_fusion, pred[512]{0:T(512)(128)(4,1)S(1)} %get-tuple-element.9), kind=kOutput, calls=%fused_computation.31 | convolution fusion | flops 6450839552 | bytes 50334208 | tf_op jit(solution)/shard_map/ktc,trc->ktr/dot_general | solution.py:26
  131.0 51.8 %scatter_fusion = f32[64,64,128]{2,0,1:T(8,128)S(1)} fusion(f32[64,64,128]{2,0,1:T(8,128)S(1)} %broadcast.100.clone.2, s32[512]{0:T(512)S(1)} %bitcast.125, f32[512,64,128]{2,1,0:T(8,128)} %broadcast_multiply_fusion.3), kind=kCustom, calls=%fused_computation.4 | custom fusion | flops 4194304 | bytes 50333696 | tf_op jit(solution)/shard_map/scatter-add | solution.py:34
  184.4 28.8 %reduce-scatter.5.cloned.1.call-done = f32[64,2048]{1,0:T(8,128)} async-done(((f32[64,8192]{1,0:T(8,128)}), f32[64,2048]{1,0:T(8,128)}) %reduce-scatter.5.cloned.1.call-update) | async-done | bytes 524304 | tf_op jit(solution)/shard_map/reduce_scatter | solution.py:74
  215.1 66.2 %psum.28 = f32[64,64]{0,1:T(8,128)S(1)} all-reduce(f32[64,64]{0,1:T(8,128)S(1)} %fusion.45), channel_id=1, replica_groups=mesh['users'=32,'items'=4] {'users','items'}, use_global_device_ids=true, to_apply=%region_2.4 | all-reduce | flops 4096 | bytes 32768 | tf_op jit(solution)/shard_map/psum | solution.py:77
  281.3 5.8 cholesky.74
  288.5 4.9 custom-call.10
  296.0 26.3 %all-gather.7.cloned.1.call-done = f32[64,8192]{1,0:T(8,128)} async-done(((f32[64,2048]{1,0:T(8,128)}), f32[64,8192]{1,0:T(8,128)}) %all-gather.7.cloned.1.call-update) | async-done | bytes 2097168 | tf_op jit(solution)/shard_map/all_gather | solution.py:79
  324.2 7.0 gather_fusion.1
  331.2 22.0 %broadcast_multiply_fusion.2 = f32[512,64,128]{2,1,0:T(8,128)} fusion(f32[512]{0:T(512)S(1)} %get-tuple-element.8, bf16[1,1,512,128,128]{4,3,2,1,0:T(8,128)(2,1)} %param.17, f32[512,64,128]{2,1,0:T(8,128)} %gather_fusion.1, pred[512]{0:T(512)(128)(4,1)S(1)} %compare_and_fusion.1), kind=kOutput, calls=%fused_computation.30 | convolution fusion | flops 6450839552 | bytes 50334208 | tf_op jit(solution)/shard_map/ktr,trc->ktc/dot_general | solution.py:40
  353.5 51.8 %scatter_fusion.1 = f32[64,64,128]{2,0,1:T(8,128)S(1)} fusion(f32[64,64,128]{2,0,1:T(8,128)S(1)} %broadcast.100.clone.1, s32[512]{0:T(512)S(1)} %bitcast.127, f32[512,64,128]{2,1,0:T(8,128)} %broadcast_multiply_fusion.2), kind=kCustom, calls=%fused_computation.5 | custom fusion | flops 4194304 | bytes 50333696 | tf_op jit(solution)/shard_map/scatter-add | solution.py:48
  406.9 163.3 %reduce-scatter.7.cloned.1.call-done = f32[64,256]{1,0:T(8,128)} async-done(((f32[64,8192]{1,0:T(8,128)}), f32[64,256]{1,0:T(8,128)}) %reduce-scatter.7.cloned.1.call-update) | async-done | bytes 65552 | tf_op jit(solution)/shard_map/reduce_scatter | solution.py:81
  571.3 87.1 %psum.29 = f32[64,64]{0,1:T(8,128)S(1)} all-reduce(f32[64,64]{0,1:T(8,128)S(1)} %fusion.56), channel_id=1, replica_groups=mesh['users'=32,'items'=4] {'users','items'}, use_global_device_ids=true, to_apply=%region_7.0 | all-reduce | flops 4096 | bytes 32768 | tf_op jit(solution)/shard_map/psum | solution.py:84
  658.5 5.8 cholesky.85
  665.7 4.9 custom-call.11
  672.4 66.5 %all-gather.9.cloned.1.call-done = f32[64,8192]{1,0:T(8,128)} async-done(((f32[64,256]{1,0:T(8,128)}), f32[64,8192]{1,0:T(8,128)}) %all-gather.9.cloned.1.call-update) | async-done | bytes 2097168 | tf_op jit(solution)/shard_map/all_gather | solution.py:53
  740.8 7.0 gather_fusion.2
  747.8 37.3 %broadcast_multiply_fusion.1 = f32[512,64,128]{2,1,0:T(8,128)} fusion(f32[512]{0:T(512)S(1)} %get-tuple-element.8, bf16[1,1,512,128,128]{4,3,2,1,0:T(8,128)(2,1)} %param.17, f32[512,64,128]{2,1,0:T(8,128)} %gather_fusion.2, pred[512]{0:T(512)(128)(4,1)S(1)} %get-tuple-element.9), kind=kOutput, calls=%fused_computation.29 | convolution fusion | flops 6450839552 | bytes 50334208 | tf_op jit(solution)/shard_map/ktc,trc->ktr/dot_general | solution.py:26
  785.3 51.8 %scatter_fusion.2 = f32[64,64,128]{2,0,1:T(8,128)S(1)} fusion(f32[64,64,128]{2,0,1:T(8,128)S(1)} %broadcast.100.clone, s32[512]{0:T(512)S(1)} %bitcast.126, f32[512,64,128]{2,1,0:T(8,128)} %broadcast_multiply_fusion.1), kind=kCustom, calls=%fused_computation.6 | custom fusion | flops 4194304 | bytes 50333696 | tf_op jit(solution)/shard_map/scatter-add | solution.py:34
  838.7 28.8 %reduce-scatter.9.cloned.1.call-done = f32[64,2048]{1,0:T(8,128)} async-done(((f32[64,8192]{1,0:T(8,128)}), f32[64,2048]{1,0:T(8,128)}) %reduce-scatter.9.cloned.1.call-update) | async-done | bytes 524304 | tf_op jit(solution)/shard_map/reduce_scatter | solution.py:74
  869.4 66.3 %psum.30 = f32[64,64]{0,1:T(8,128)S(1)} all-reduce(f32[64,64]{0,1:T(8,128)S(1)} %fusion.42), channel_id=1, replica_groups=mesh['users'=32,'items'=4] {'users','items'}, use_global_device_ids=true, to_apply=%region_10.15 | all-reduce | flops 4096 | bytes 32768 | tf_op jit(solution)/shard_map/psum | solution.py:77
  935.7 5.8 cholesky.96
  942.9 4.9 custom-call.12
  950.5 26.4 %all-gather.11.cloned.1.call-done = f32[64,8192]{1,0:T(8,128)} async-done(((f32[64,2048]{1,0:T(8,128)}), f32[64,8192]{1,0:T(8,128)}) %all-gather.11.cloned.1.call-update) | async-done | bytes 2097168 | tf_op jit(solution)/shard_map/all_gather | solution.py:79
  978.8 7.0 gather_fusion.3
  985.8 22.0 %broadcast_multiply_fusion = f32[512,64,128]{2,1,0:T(8,128)} fusion(f32[512]{0:T(512)S(1)} %get-tuple-element.8, bf16[1,1,512,128,128]{4,3,2,1,0:T(8,128)(2,1)} %param.17, f32[512,64,128]{2,1,0:T(8,128)} %gather_fusion.3, pred[512]{0:T(512)(128)(4,1)S(1)} %compare_and_fusion.1), kind=kOutput, calls=%fused_computation.28 | convolution fusion | flops 6450839552 | bytes 50334208 | tf_op jit(solution)/shard_map/ktr,trc->ktc/dot_general | solution.py:40
  1008.0 51.8 %scatter_fusion.3 = f32[64,64,128]{2,0,1:T(8,128)S(1)} fusion(f32[64,64,128]{2,0,1:T(8,128)S(1)} %broadcast.100, s32[512]{0:T(512)S(1)} %bitcast.128, f32[512,64,128]{2,1,0:T(8,128)} %broadcast_multiply_fusion), kind=kCustom, calls=%fused_computation.7 | custom fusion | flops 4194304 | bytes 50333696 | tf_op jit(solution)/shard_map/scatter-add | solution.py:48
  1061.4 163.4 %reduce-scatter.11.cloned.1.call-done = f32[64,256]{1,0:T(8,128)} async-done(((f32[64,8192]{1,0:T(8,128)}), f32[64,256]{1,0:T(8,128)}) %reduce-scatter.11.cloned.1.call-update) | async-done | bytes 65552 | tf_op jit(solution)/shard_map/reduce_scatter | solution.py:81
  1225.9 87.0 %psum.31 = f32[64,64]{0,1:T(8,128)S(1)} all-reduce(f32[64,64]{0,1:T(8,128)S(1)} %fusion.53), channel_id=1, replica_groups=mesh['users'=32,'items'=4] {'users','items'}, use_global_device_ids=true, to_apply=%region_13.18 | all-reduce | flops 4096 | bytes 32768 | tf_op jit(solution)/shard_map/psum | solution.py:84
  1313.0 5.8 cholesky.107
  1320.2 4.9 custom-call.13
  (77 shorter events, 39.1 us)
Async XLA Ops:
  7.2 77.4 %all-gather.5.cloned.1.call-start = ((), (), s32[]{:S(2)}) async-start(), calls=%async_computation.4 | async-start | bytes 2162688 | tf_op jit(solution)/shard_map/all_gather | solution.py:53
  9.3 203.9 %reduce-scatter.5.cloned.1.call-start = ((), (), s32[]{:S(2)}) async-start(), calls=%async_computation.5 | async-start | bytes 2621440 | tf_op jit(solution)/shard_map/reduce_scatter | solution.py:74
  131.0 53.4 %copy-start.2 = (s32[2048]{0:T(1024)S(1)}, s32[2048]{0:T(1024)}, u32[]{:S(2)}) copy-start(s32[2048]{0:T(1024)} %param.18) | copy-start | bytes 24580
  131.0 165.0 %copy-start = (s32[1,1,512]{2,1,0:T(1,128)S(1)}, s32[1,1,512]{2,1,0:T(1,128)}, u32[]{:S(2)}) copy-start(s32[1,1,512]{2,1,0:T(1,128)} %param.14) | copy-start | bytes 6148
  131.0 165.0 %copy-start.1 = (s32[1,1,512]{2,1,0:T(1,128)S(1)}, s32[1,1,512]{2,1,0:T(1,128)}, u32[]{:S(2)}) copy-start(s32[1,1,512]{2,1,0:T(1,128)} %param.15) | copy-start | bytes 6148
  184.4 138.0 %all-gather.7.cloned.1.call-start = ((), (), s32[]{:S(2)}) async-start(), calls=%async_computation.6 | async-start | bytes 2621440 | tf_op jit(solution)/shard_map/all_gather | solution.py:79
  295.9 274.3 %reduce-scatter.7.cloned.1.call-start = ((), (), s32[]{:S(2)}) async-start(), calls=%async_computation.7 | async-start | bytes 2162688 | tf_op jit(solution)/shard_map/reduce_scatter | solution.py:81
  406.8 332.1 %all-gather.9.cloned.1.call-start = ((), (), s32[]{:S(2)}) async-start(), calls=%async_computation.8 | async-start | bytes 2162688 | tf_op jit(solution)/shard_map/all_gather | solution.py:53
  672.4 195.2 %reduce-scatter.9.cloned.1.call-start = ((), (), s32[]{:S(2)}) async-start(), calls=%async_computation.9 | async-start | bytes 2621440 | tf_op jit(solution)/shard_map/reduce_scatter | solution.py:74
  838.7 138.2 %all-gather.11.cloned.1.call-start = ((), (), s32[]{:S(2)}) async-start(), calls=%async_computation.10 | async-start | bytes 2621440 | tf_op jit(solution)/shard_map/all_gather | solution.py:79
  950.5 274.3 %reduce-scatter.11.cloned.1.call-start = ((), (), s32[]{:S(2)}) async-start(), calls=%async_computation.11 | async-start | bytes 2162688 | tf_op jit(solution)/shard_map/reduce_scatter | solution.py:81
Sparse Core Ops, SparseCore 0:
  11.3 73.1 all-gather.4
  184.5 28.7 reduce-scatter.4
  296.0 26.2 all-gather.6
  406.9 163.1 reduce-scatter.6
  672.5 66.3 all-gather.8
  838.8 28.7 reduce-scatter.8
  950.6 26.2 all-gather.10
  1061.5 163.1 reduce-scatter.10
where the time goes:
time: 1350 us; the launch traced here: 1330 us
  waiting for transfers between devices  576 us (43%)
  blocking collectives  307 us (23%)
  other arithmetic  260 us (19%)
  matrix products  133 us (10%)
  local copies, waits for them, and re-layouts  42.5 us (3%)
  between operations  15.6 us (1%)
    reduce_scatter x2, waiting for transfers between devices, body(): lax.psum_scatter(partial_items, 'users', scatter_dimension=1, tiled=True)  327 us
    psum x2, blocking collectives, body(): item_gram = lax.psum(local_gram(item_raw), ('users', 'items'))  174 us
    all_gather x2, waiting for transfers between devices, gather_items(): return lax.all_gather(sent, 'users', axis=1, tiled=True)  139 us
    psum x2, blocking collectives, body(): user_gram = lax.psum(local_gram(user_raw), ('users', 'items'))  132 us
    scatter-add x2, other arithmetic, item_partial(): summed = jnp.zeros((K, IT, TILE), jnp.float32).at[:, cols, :].add(product)  104 us
    scatter-add x2, other arithmetic, user_partial(): summed = jnp.zeros((K, UT, TILE), jnp.float32).at[:, rows, :].add(product)  104 us
    dot_general x2, matrix products, user_partial(): jnp.einsum('ktc,trc->ktr', picked, values, precision=lax.Precision.HIGHES...  74.6 us
    reduce_scatter x2, waiting for transfers between devices, body(): lax.psum_scatter(partial_users, 'items', scatter_dimension=1, tiled=True)  57.7 us
  transfers between devices with their start and end apart: 8, of which 8 were waited for; matrix products, arithmetic and copies ran while one was open for 0% of the time, Pallas kernels for 0%

commit v1 on v0

v1 whole, which is shorter than its diff:
```python
import functools

import jax
import jax.numpy as jnp
from jax import lax
from jax.experimental import pallas as pl
from jax.experimental.pallas import tpu as pltpu
from jax.sharding import PartitionSpec as P

K = 64
H = K // 2
Q = K // 4
TILE = 128
UT = 64
IT = 64
CHUNK = 64
UNROLL = 8
NCH = 4
MESH = pl.DeviceIdType.MESH
F32 = jnp.float32
HIGHEST = lax.Precision.HIGHEST
VMEM_LIMIT = 56 * 1024 * 1024
VMEM = pl.BlockSpec(memory_space=pltpu.VMEM)


def tile_products(contract, count_s, from_s, to_s, full_ref, vals_ref, out_ref, split):
    g = pl.program_id(0)

    @pl.when(g == 0)
    def _():
        def prepare(i, carry):
            x = full_ref[i]
            high = x.astype(jnp.bfloat16)
            split[i, :K] = high
            split[i, K:] = (x - high.astype(F32)).astype(jnp.bfloat16)
            out_ref[i] = jnp.zeros((K, TILE), F32)
            return carry

        lax.fori_loop(0, IT, prepare, 0)

    count = count_s[0]
    live = jnp.clip(count - g * CHUNK, 0, CHUNK)

    def group(j, carry):
        base = j * UNROLL
        products = []
        for q in range(UNROLL):
            both = lax.dot_general(
                split[from_s[g * CHUNK + base + q]],
                vals_ref[base + q],
                (((1,), (contract,)), ((), ())),
                preferred_element_type=F32,
            )
            products.append(jnp.where(base + q < live, both[:K] + both[K:], 0.0))
        for q in range(UNROLL):
            to = to_s[g * CHUNK + base + q]
            out_ref[to] = out_ref[to] + products[q]
        return carry

    lax.fori_loop(0, (live + UNROLL - 1) // UNROLL, group, 0)


def products_call(contract, count, source, target, full, vals):
    slots = vals.shape[0]
    whole = pl.BlockSpec((UT, K, TILE), lambda g, n, a, b: (0, 0, 0))
    return pl.pallas_call(
        functools.partial(tile_products, contract),
        out_shape=jax.ShapeDtypeStruct((UT, K, TILE), F32),
        grid_spec=pltpu.PrefetchScalarGridSpec(
            num_scalar_prefetch=3,
            grid=(slots // CHUNK,),
            in_specs=[
                whole,
                pl.BlockSpec(
                    (CHUNK, TILE, TILE),
                    lambda g, n, a, b: (jnp.minimum(g, (n[0] - 1) // CHUNK), 0, 0),
                ),
            ],
            out_specs=whole,
            scratch_shapes=[pltpu.VMEM((UT, 2 * K, TILE), jnp.bfloat16)],
        ),
        compiler_params=pltpu.CompilerParams(vmem_limit_bytes=VMEM_LIMIT),
        name="products_users" if contract == 1 else "products_items",
    )(count, source, target, full, vals)


class Place:
    def __init__(self):
        users = lax.axis_index("users")
        items = lax.axis_index("items")
        self.xh, self.y, self.z = users // 16, (users // 4) % 4, users % 4
        self.xl, self.core = items // 2, items % 2

    def at(self, xh=None, y=None, z=None, xl=None, core=None):
        xh = self.xh if xh is None else xh
        y = self.y if y is None else y
        z = self.z if z is None else z
        xl = self.xl if xl is None else xl
        core = self.core if core is None else core
        return ((xh * 4 + y) * 4 + z, xl * 2 + core)

    def near(self):
        out = []
        for k in range(1, 8):
            j = (self.xh * 4 + self.xl * 2 + self.core + k) % 8
            out.append(self.at(xh=j // 4, xl=(j // 2) % 2, core=j % 2))
        return out

    def plane(self):
        out = []
        for k in range(1, 16):
            j = (self.y * 4 + self.z + k) % 16
            out.append(self.at(y=j // 4, z=j % 4))
        return out


def greet(devices):
    barrier = pltpu.get_barrier_semaphore()
    for device in devices:
        pl.semaphore_signal(barrier, inc=1, device_id=device, device_id_type=MESH)
    pl.semaphore_wait(barrier, len(devices))


class Sems:
    def __init__(self, send, recv):
        self.send, self.recv, self.used = send, recv, 0

    def copy(self, src, dst, device):
        k = self.used
        self.used += 1
        return pltpu.make_async_remote_copy(
            src_ref=src,
            dst_ref=dst,
            send_sem=self.send.at[k],
            recv_sem=self.recv.at[k],
            device_id=device,
            device_id_type=MESH,
        )


LOW, HIGH = slice(0, Q), slice(Q, H)


def rows(half, part=None):
    start = half * H + (Q if part is HIGH else 0)
    return pl.ds(start, H if part is None else Q)


class RingGather:
    def __init__(self, sems, slab, me, device):
        plus, minus, far = (me + 1) % 4, (me + 3) % 4, (me + 2) % 4
        to_plus, to_minus = device(plus), device(minus)
        self.own = [
            sems.copy(slab(me, None), slab(me, None), to_plus),
            sems.copy(slab(me, None), slab(me, None), to_minus),
        ]
        self.on = [
            sems.copy(slab(minus, LOW), slab(minus, LOW), to_plus),
            sems.copy(slab(plus, HIGH), slab(plus, HIGH), to_minus),
        ]
        del far

    def start(self):
        for copy in self.own:
            copy.start()

    def forward(self):
        for own, on in zip(self.own, self.on):
            own.wait_recv()
            on.start()

    def finish(self):
        for on in self.on:
            on.wait_recv()

    def drain(self):
        for copy in self.own + self.on:
            copy.wait_send()


class RingReduce:
    def __init__(self, sems, slab, me, device, first, second, sums):
        plus, minus, far = (me + 1) % 4, (me + 3) % 4, (me + 2) % 4
        to_plus, to_minus = device(plus), device(minus)
        self.slab, self.me, self.plus, self.minus = slab, me, plus, minus
        self.first, self.second, self.sums = first, second, sums
        self.far = [
            sems.copy(slab(far, LOW), first.at[0], to_plus),
            sems.copy(slab(far, HIGH), first.at[1], to_minus),
        ]
        self.plain = [
            sems.copy(slab(plus, HIGH), second.at[0, 1], to_plus),
            sems.copy(slab(minus, LOW), second.at[1, 0], to_minus),
        ]
        self.summed = [
            sems.copy(sums.at[0], second.at[0, 0], to_plus),
            sems.copy(sums.at[1], second.at[1, 1], to_minus),
        ]

    def start(self):
        for copy in self.far + self.plain:
            copy.start()

    def forward(self):
        for k, (place, part) in enumerate(((self.plus, LOW), (self.minus, HIGH))):
            self.far[k].wait_recv()
            self.sums[k] = self.slab(place, part)[...] + self.first[k]
            self.summed[k].start()

    def finish(self, out_low, out_high):
        self.plain[1].wait_recv()
        self.summed[0].wait_recv()
        out_low[...] = self.slab(self.me, LOW)[...] + (self.second[0, 0] + self.second[1, 0])
        self.plain[0].wait_recv()
        self.summed[1].wait_recv()
        out_high[...] = self.slab(self.me, HIGH)[...] + (self.second[0, 1] + self.second[1, 1])

    def drain(self):
        for copy in self.far + self.plain + self.summed:
            copy.wait_send()


class GramSum:
    def __init__(self, sems, place, near_buf, plane_buf):
        self.near_buf, self.plane_buf = near_buf, plane_buf
        self.n = place.xh * 4 + place.xl * 2 + place.core
        self.p = place.y * 4 + place.z
        self.near = [sems.copy(near_buf.at[self.n], near_buf.at[self.n], d) for d in place.near()]
        self.plane = [sems.copy(plane_buf.at[self.p], plane_buf.at[self.p], d) for d in place.plane()]

    def start(self, value):
        self.near_buf[self.n] = value
        for copy in self.near:
            copy.start()

    def forward(self):
        for copy in self.near:
            copy.wait_recv()
        total = self.near_buf[0]
        for k in range(1, 8):
            total = total + self.near_buf[k]
        self.plane_buf[self.p] = total
        for copy in self.plane:
            copy.start()

    def finish(self):
        for copy in self.plane:
            copy.wait_recv()
        total = self.plane_buf[0]
        for k in range(1, 16):
            total = total + self.plane_buf[k]
        return total

    def drain(self):
        for copy in self.near + self.plane:
            copy.wait_send()


def inverse_factor(gram):
    row = lax.broadcasted_iota(jnp.int32, (K, 2 * K), 0)
    lane = lax.broadcasted_iota(jnp.int32, (K, 2 * K), 1)
    work = jnp.concatenate([gram, jnp.zeros((K, K), F32)], axis=1)
    work = work + jnp.where(lane == row + K, 1.0, 0.0)
    for j in range(K):
        scale = lax.rsqrt(work[j : j + 1, j : j + 1])
        pivot = work[j : j + 1, :] * scale
        column = work[:, j : j + 1] * scale
        work = jnp.where(row > j, work - column * pivot, jnp.where(row == j, pivot, work))
    return work[:, K:]


def apply(left, right):
    return jnp.dot(left, right, precision=HIGHEST, preferred_element_type=F32)


def gram_of(tiles):
    total = jnp.zeros((K, K), F32)
    for x in tiles:
        total = total + lax.dot_general(
            x, x, (((1,), (1,)), ((), ())), precision=HIGHEST, preferred_element_type=F32
        )
    return total


def gather_rings(sems, place, full):
    def along_y(half, whole):
        if whole:
            slab = lambda n, part: full.at[:, n, :, :, rows(half, part)]
        else:
            slab = lambda n, part: full.at[:, n, place.z, :, rows(half, part)]
        return RingGather(sems, slab, place.y, lambda n: place.at(y=n))

    def along_z(half, whole):
        if whole:
            slab = lambda n, part: full.at[:, :, n, :, rows(half, part)]
        else:
            slab = lambda n, part: full.at[:, place.y, n, :, rows(half, part)]
        return RingGather(sems, slab, place.z, lambda n: place.at(z=n))

    return [along_y(0, False), along_z(1, False)], [along_z(0, True), along_y(1, True)]


def across_x(sems, place, full):
    own = full.at[place.xh, place.y, place.z]
    return sems.copy(own, own, place.at(xh=1 - place.xh))


def gather_kernel(sent_ref, full, send, recv):
    place = Place()
    sems = Sems(send, recv)
    cross = across_x(sems, place, full)
    first, second = gather_rings(sems, place, full)
    greet(
        [place.at(xh=1 - place.xh)]
        + [place.at(y=(place.y + k) % 4) for k in (1, 3)]
        + [place.at(z=(place.z + k) % 4) for k in (1, 3)]
    )
    full[place.xh, place.y, place.z] = sent_ref[...]
    cross.start()
    cross.wait_recv()
    for step in ("start", "forward"):
        for ring in first:
            getattr(ring, step)()
    for ring, later in zip(first, second):
        ring.finish()
        later.start()
    for step in ("forward", "finish"):
        for ring in second:
            getattr(ring, step)()
    cross.wait_send()
    for ring in first + second:
        ring.drain()


def remote_call(kernel, name, collective_id, out_shape, scratch_shapes, copies, *args):
    return pl.pallas_call(
        kernel,
        out_shape=out_shape,
        in_specs=[VMEM] * len(args),
        out_specs=jax.tree.map(lambda _: VMEM, out_shape),
        scratch_shapes=[
            *scratch_shapes,
            pltpu.SemaphoreType.DMA((copies,)),
            pltpu.SemaphoreType.DMA((copies,)),
        ],
        compiler_params=pltpu.CompilerParams(
            collective_id=collective_id, has_side_effects=True, vmem_limit_bytes=VMEM_LIMIT
        ),
        name=name,
    )(*args)


FULL = (2, 4, 4, 2, K, TILE)


def gather_call(sent):
    return remote_call(
        gather_kernel, "items_gather", 1, jax.ShapeDtypeStruct(FULL, F32), [], 17, sent
    )


def reduce_scratch():
    out = []
    for lead in ((2, 4, 2), (2, 4, 2), (2, 2), (2, 2)):
        out += [
            pltpu.VMEM((2, *lead, Q, TILE), F32),
            pltpu.VMEM((2, 2, *lead, Q, TILE), F32),
            pltpu.VMEM((2, *lead, Q, TILE), F32),
        ]
    return out + [
        pltpu.VMEM((2, 4, 2, H, TILE), F32),
        pltpu.VMEM((2, 4, 2, H, TILE), F32),
        pltpu.VMEM((2, 2, K, TILE), F32),
        pltpu.VMEM((2, K, TILE), F32),
    ]


REDUCE_SCRATCH = 16


def reduce_rings(sems, place, partial, bufs):
    half0, half1, mine, arrived = bufs[12:16]
    part = lambda p: slice(0, H) if p is None else p
    first = [
        RingReduce(sems, lambda n, p: partial.at[:, :, n, :, rows(0, p)], place.z,
                   lambda n: place.at(z=n), *bufs[0:3]),
        RingReduce(sems, lambda n, p: partial.at[:, n, :, :, rows(1, p)], place.y,
                   lambda n: place.at(y=n), *bufs[3:6]),
    ]
    second = [
        RingReduce(sems, lambda n, p: half0.at[:, n, :, part(p)], place.y,
                   lambda n: place.at(y=n), *bufs[6:9]),
        RingReduce(sems, lambda n, p: half1.at[:, n, :, part(p)], place.z,
                   lambda n: place.at(z=n), *bufs[9:12]),
    ]
    outs = [
        [half0.at[:, :, :, LOW], half0.at[:, :, :, HIGH]],
        [half1.at[:, :, :, LOW], half1.at[:, :, :, HIGH]],
        [mine.at[:, :, rows(0, LOW)], mine.at[:, :, rows(0, HIGH)]],
        [mine.at[:, :, rows(1, LOW)], mine.at[:, :, rows(1, HIGH)]],
    ]
    cross = sems.copy(mine.at[1 - place.xh], arrived, place.at(xh=1 - place.xh))
    return first, second, outs, cross, mine, arrived


def reduced(place, first, second, outs, cross, mine, arrived, gram):
    for ring in first:
        ring.start()
    for ring in first:
        ring.forward()
    gram.forward()
    for ring, later, out in zip(first, second, outs):
        ring.finish(*out)
        later.start()
    for ring in second:
        ring.forward()
    total = gram.finish()
    for ring, out in zip(second, outs[2:]):
        ring.finish(*out)
    cross.start()
    return total


def middle_kernel(user_total, item_total, partial, gram_ref, scale_ref, full, factor_ref, *scratch):
    bufs, (near1, plane1, near2, plane2, send, recv) = scratch[:REDUCE_SCRATCH], scratch[REDUCE_SCRATCH:]
    place = Place()
    sems = Sems(send, recv)
    first, second, outs, cross, mine, arrived = reduce_rings(sems, place, partial, bufs)
    gram1 = GramSum(sems, place, near1, plane1)
    gram2 = GramSum(sems, place, near2, plane2)
    spread = across_x(sems, place, full)
    gather1, gather2 = gather_rings(sems, place, full)
    greet(place.near() + place.plane())

    gram1.start(gram_ref[...])
    total = reduced(place, first, second, outs, cross, mine, arrived, gram1)
    inverse = inverse_factor(total / user_total)
    cross.wait_recv()
    raw = [
        apply(inverse, scale_ref[t : t + 1] * (mine[place.xh, t] + arrived[t])) for t in range(2)
    ]
    for t in range(2):
        full[place.xh, place.y, place.z, t] = scale_ref[t : t + 1] * raw[t]
    spread.start()
    gram2.start(gram_of(raw))
    spread.wait_recv()
    for ring in gather1:
        ring.start()
    gram2.forward()
    for ring in gather1:
        ring.forward()
    for ring, later in zip(gather1, gather2):
        ring.finish()
        later.start()
    for ring in gather2:
        ring.forward()
    factor_ref[...] = inverse_factor(gram2.finish() / item_total)
    for ring in gather2:
        ring.finish()
    cross.wait_send()
    spread.wait_send()
    for part in first + second + gather1 + gather2 + [gram1, gram2]:
        part.drain()


GRAM_SCRATCH = [pltpu.VMEM((8, K, K), F32), pltpu.VMEM((16, K, K), F32)]


def middle_call(user_total, item_total, partial, gram, scale):
    return remote_call(
        functools.partial(middle_kernel, user_total, item_total),
        "items_reduce_gather",
        2,
        (jax.ShapeDtypeStruct(FULL, F32), jax.ShapeDtypeStruct((K, K), F32)),
        reduce_scratch() + GRAM_SCRATCH * 2,
        24 + 1 + 44 + 17,
        partial,
        gram,
        scale,
    )


def last_kernel(
    user_total, item_total, partial, gram_ref, scale_ref, factor_ref, users_ref, user_out, item_out, *scratch
):
    bufs, (near1, plane1, near2, plane2, send, recv) = scratch[:REDUCE_SCRATCH], scratch[REDUCE_SCRATCH:]
    place = Place()
    sems = Sems(send, recv)
    first, second, outs, cross, mine, arrived = reduce_rings(sems, place, partial, bufs)
    gram1 = GramSum(sems, place, near1, plane1)
    gram2 = GramSum(sems, place, near2, plane2)
    greet(place.near() + place.plane())

    gram1.start(gram_ref[...])
    total = reduced(place, first, second, outs, cross, mine, arrived, gram1)
    inverse = inverse_factor(total / user_total)
    cross.wait_recv()
    raw = [
        apply(inverse, apply(factor_ref[...], scale_ref[t : t + 1] * (mine[place.xh, t] + arrived[t])))
        for t in range(2)
    ]
    gram2.start(gram_of(raw))
    for t in range(8):
        user_out[:, t * TILE : (t + 1) * TILE] = apply(inverse, users_ref[t])
    gram2.forward()
    for t in range(8, 16):
        user_out[:, t * TILE : (t + 1) * TILE] = apply(inverse, users_ref[t])
    inverse2 = inverse_factor(gram2.finish() / item_total)
    for t in range(2):
        item_out[:, t * TILE : (t + 1) * TILE] = apply(inverse2, raw[t])
    cross.wait_send()
    for part in first + second + [gram1, gram2]:
        part.drain()


def last_call(user_total, item_total, partial, gram, scale, factor, users):
    return remote_call(
        functools.partial(last_kernel, user_total, item_total),
        "items_reduce_last",
        3,
        (jax.ShapeDtypeStruct((K, 16 * TILE), F32), jax.ShapeDtypeStruct((K, 2 * TILE), F32)),
        reduce_scratch() + GRAM_SCRATCH * 2,
        24 + 1 + 44,
        partial,
        gram,
        scale,
        factor,
        users,
    )


def users_kernel(with_factor, *refs):
    if with_factor:
        partial, scale_ref, factor_ref, *refs = refs
    else:
        partial, scale_ref, *refs = refs
    full, raw_ref, gram_ref, from_core, from_chip, sums, send, recv = refs
    place = Place()
    sems = Sems(send, recv)
    xl, core = place.xl, place.core
    size = 16 // NCH
    sibling = place.at(core=1 - core)
    partner = place.at(xl=1 - xl)

    def tiles(xq, cq, j):
        return pl.ds((xq * 2 + cq) * 16 + j * size, size)

    def to_core(xq, slot):
        return [
            sems.copy(partial.at[tiles(xq, 1 - core, j)], from_core.at[slot, j], sibling) for j in range(NCH)
        ]

    core_other, core_mine = to_core(1 - xl, 0), to_core(xl, 1)
    to_chip = [sems.copy(sums.at[j], from_chip.at[j], partner) for j in range(NCH)]
    mine = [full.at[tiles(xl, core, j)] for j in range(NCH)]
    theirs = [full.at[tiles(1 - xl, core, j)] for j in range(NCH)]
    done_chip = [sems.copy(mine[j], mine[j], partner) for j in range(NCH)]
    done_core = [sems.copy(mine[j], mine[j], sibling) for j in range(NCH)]
    passed = [sems.copy(theirs[j], theirs[j], sibling) for j in range(NCH)]
    greet([sibling, partner])

    for copy in core_other + core_mine:
        copy.start()
    for j in range(NCH):
        core_other[j].wait_recv()
        sums[j] = partial[tiles(1 - xl, core, j)] + from_core[0, j]
        to_chip[j].start()
    for j in range(NCH):
        core_mine[j].wait_recv()
        to_chip[j].wait_recv()
        for t in range(size):
            row = j * size + t
            scale = scale_ref[row : row + 1]
            place_t = (xl * 2 + core) * 16 + row
            raw = scale * (partial[place_t] + (from_core[1, j, t] + from_chip[j, t]))
            full[place_t] = scale * raw
            raw_ref[row] = raw
        done_chip[j].start()
        done_core[j].start()
    if with_factor:
        for t in range(16):
            raw_ref[t] = apply(factor_ref[...], raw_ref[t])
    gram_ref[...] = gram_of([raw_ref[t] for t in range(16)])
    for j in range(NCH):
        done_chip[j].wait_recv()
        passed[j].start()
    for j in range(NCH):
        done_core[j].wait_recv()
        passed[j].wait_recv()
    for copy in core_other + core_mine + to_chip + done_chip + done_core + passed:
        copy.wait_send()


def users_call(partial, scale, factor=None):
    size = 16 // NCH
    return remote_call(
        functools.partial(users_kernel, factor is not None),
        "users_sum" if factor is None else "users_sum_again",
        4 if factor is None else 5,
        (
            jax.ShapeDtypeStruct((UT, K, TILE), F32),
            jax.ShapeDtypeStruct((16, K, TILE), F32),
            jax.ShapeDtypeStruct((K, K), F32),
        ),
        [
            pltpu.VMEM((2, NCH, size, K, TILE), F32),
            pltpu.VMEM((NCH, size, K, TILE), F32),
            pltpu.VMEM((NCH, size, K, TILE), F32),
        ],
        6 * NCH,
        partial,
        scale,
        *([] if factor is None else [factor]),
    )


def body(tile_rows, tile_cols, tile_count, tile_vals, user_degree, item_degree, start_items):
    tile_row, tile_col, count = tile_rows[0, 0], tile_cols[0, 0], tile_count[0]
    vals = tile_vals[0, 0]
    user_scale = lax.rsqrt(user_degree.astype(F32)).reshape(16, TILE)
    item_scale = lax.rsqrt(item_degree.astype(F32)).reshape(2, TILE)
    user_total = 16 * TILE * lax.axis_size("users") * lax.axis_size("items")
    item_total = 2 * TILE * lax.axis_size("users") * lax.axis_size("items")
    sent = item_scale[:, None, :] * start_items.astype(F32).reshape(K, 2, TILE).transpose(1, 0, 2)

    full_items = gather_call(sent)
    partial = products_call(1, count, tile_col, tile_row, full_items.reshape(IT, K, TILE), vals)
    full_users, _, gram = users_call(partial, user_scale)
    partial = products_call(0, count, tile_row, tile_col, full_users, vals)
    full_items, factor = middle_call(user_total, item_total, partial.reshape(FULL), gram, item_scale)
    partial = products_call(1, count, tile_col, tile_row, full_items.reshape(IT, K, TILE), vals)
    full_users, raw, gram = users_call(partial, user_scale, factor)
    partial = products_call(0, count, tile_row, tile_col, full_users, vals)
    return last_call(user_total, item_total, partial.reshape(FULL), gram, item_scale, factor, raw)


def solution(mesh):
    in_specs = (
        P("users", "items", None),
        P("users", "items", None),
        P("users", "items"),
        P("users", "items", None, None, None),
        P(("users", "items")),
        P(("items", "users")),
        P(None, ("items", "users")),
    )
    out_specs = (P(None, ("users", "items")), P(None, ("items", "users")))
    return jax.shard_map(body, mesh=mesh, in_specs=in_specs, out_specs=out_specs, check_vma=False)
```

time: 1350 us -> 316 us (0.23); the launches traced: 1330 us -> 315 us
  waiting for transfers between devices: 576 us -> 0 us
  Pallas kernels: 0 us -> 307 us
  blocking collectives: 307 us -> 0 us
  other arithmetic: 260 us -> 3.38 us
  matrix products: 133 us -> 0 us
  local copies, waits for them, and re-layouts: 42.5 us -> 3.35 us
  between operations: 15.6 us -> 1.32 us
    reduce_scatter x4 -> x0, waiting for transfers between devices: 384 us -> none  [the longest x2 327 us: body(): lax.psum_scatter(partial_items, 'users', scatter_dimension=1, tiled=True)]
    pallas_call x0 -> x9, Pallas kernels: none -> 307 us  [the longest x5 278 us: remote_call(): pl.pallas_call(kernel, out_shape=out_shape, in_specs=[VMEM] * len(args),...]
    psum x4 -> x0, blocking collectives: 307 us -> none  [the longest x2 174 us: body(): item_gram = lax.psum(local_gram(item_raw), ('users', 'items'))]
    scatter-add x4 -> x0, other arithmetic: 207 us -> none  [the longest x2 104 us: item_partial(): summed = jnp.zeros((K, IT, TILE), jnp.float32).at[:, cols, :].add(product)]
    all_gather x4 -> x0, waiting for transfers between devices: 192 us -> none  [the longest x2 139 us: gather_items(): return lax.all_gather(sent, 'users', axis=1, tiled=True)]
    dot_general x8 -> x0, matrix products: 125 us -> none  [the longest x2 74.6 us: user_partial(): jnp.einsum('ktc,trc->ktr', picked, values, precision=lax.Precision.HIGHES...]
    another operation x20 -> x0, other arithmetic: 48.3 us -> none  [the longest x12 26.1 us: solve_panel(): lower = jnp.linalg.cholesky(gram)]
    gather x4 -> x0, local copies, waits for them, and re-layouts: 27.9 us -> none  [the longest x2 13.9 us: user_partial(): picked = jnp.take(full_items.reshape(K, IT, TILE), cols, axis=1)]
  transfers between devices with their start and end apart: 8 -> 0, of which waited for: 8 -> 0; matrix products, arithmetic and copies ran while one was open for 0% -> 0% of each run, Pallas kernels for 0% -> 0%
where the time goes in v1:
time: 316 us; the launch traced here: 315 us
  Pallas kernels  307 us (97%)
  other arithmetic  3.38 us (1%)
  local copies, waits for them, and re-layouts  3.35 us (1%)
    pallas_call x5, Pallas kernels, remote_call(): pl.pallas_call(kernel, out_shape=out_shape, in_specs=[VMEM] * len(args),...  278 us
    pallas_call x4, Pallas kernels, products_call(): pl.pallas_call(functools.partial(tile_products, contract), out_shape=jax....  29 us

profile of v1, /device:TPU:1, one launch (start us, length us, event | category | flops | bytes accessed | tf_op | source)
XLA Modules:
  0.0 315.4 jit_solution(8608705863107494660)
XLA Ops:
  1.3 0.7 rsqrt_bitcast_fusion.1.scale_ref
  2.0 0.0 copy-start
  2.0 1.3 rsqrt_bitcast_fusion.refs_1_
  3.3 1.4 fusion.sent_ref
  4.7 29.1 %items_gather.1 = f32[2,4,4,2,64,128]{5,4,3,2,1,0:T(8,128)} custom-call(f32[2,64,128]{2,1,0:T(8,128)} %fusion.sent_ref), custom_call_target="tpu_custom_call" | custom-call | tf_op jit(solution)/shard_map/items_gather/pallas_call | solution.py:336
  33.7 7.6 %products_users.2.refs_0_ = f32[64,64,128]{2,1,0:T(8,128)} custom-call(s32[1]{0:T(128)} %bitcast.21.count_s, s32[512]{0:T(512)} %bitcast.37, s32[512]{0:T(512)} %bitcast.33, f32[64,64,128]{2,1,0:T(8,128)} %bitcast.31, bf16[512,128,128]{2,1,0:T(8,128)(2,1)} %bitcast.25), custom_call_target="tpu_custom_call" | custom-call | tf_op jit(solution)/shard_map/products_users/pallas_call | solution.py:66
  41.3 0.0 copy-done
  41.3 41.3 %users_sum.1 = (f32[64,64,128]{2,1,0:T(8,128)}, f32[16,64,128]{2,1,0:T(8,128)}, f32[64,64]{1,0:T(8,128)}) custom-call(f32[64,64,128]{2,1,0:T(8,128)} %products_users.2.refs_0_, f32[16,128]{1,0:T(8,128)} %rsqrt_bitcast_fusion.refs_1_), custom_call_target="tpu_custom_call" | custom-call | tf_op jit(solution)/shard_map/users_sum/pallas_call | solution.py:336
  82.6 6.9 %products_items.2 = f32[64,64,128]{2,1,0:T(8,128)} custom-call(s32[1]{0:T(128)} %bitcast.22.count_s, s32[512]{0:T(512)} %bitcast.34, s32[512]{0:T(512)} %bitcast.38, f32[64,64,128]{2,1,0:T(8,128)} %get-tuple-element.9.full_ref, bf16[512,128,128]{2,1,0:T(8,128)(2,1)} %bitcast.26), custom_call_target="tpu_custom_call" | custom-call | tf_op jit(solution)/shard_map/products_items/pallas_call | solution.py:66
  89.5 87.0 %items_reduce_gather.1 = (f32[2,4,4,2,64,128]{5,4,3,2,1,0:T(8,128)}, f32[64,64]{1,0:T(8,128)}) custom-call(f32[2,4,4,2,64,128]{5,4,3,2,1,0:T(8,128)} %bitcast.30, f32[64,64]{1,0:T(8,128)} %get-tuple-element.10.gram_ref, f32[2,128]{1,0:T(2,128)} %copy-done), custom_call_target="tpu_custom_call" | custom-call | tf_op jit(solution)/shard_map/items_reduce_gather/pallas_call | solution.py:336
  176.5 7.5 %products_users.3.refs_0_ = f32[64,64,128]{2,1,0:T(8,128)} custom-call(s32[1]{0:T(128)} %bitcast.23.count_s, s32[512]{0:T(512)} %bitcast.39, s32[512]{0:T(512)} %bitcast.35, f32[64,64,128]{2,1,0:T(8,128)} %bitcast.32, bf16[512,128,128]{2,1,0:T(8,128)(2,1)} %bitcast.27), custom_call_target="tpu_custom_call" | custom-call | tf_op jit(solution)/shard_map/products_users/pallas_call | solution.py:66
  184.0 40.1 %users_sum_again.1 = (f32[64,64,128]{2,1,0:T(8,128)}, f32[16,64,128]{2,1,0:T(8,128)}, f32[64,64]{1,0:T(8,128)}) custom-call(f32[64,64,128]{2,1,0:T(8,128)} %products_users.3.refs_0_, f32[16,128]{1,0:T(8,128)} %rsqrt_bitcast_fusion.refs_1_, f32[64,64]{1,0:T(8,128)} %get-tuple-element.12.refs_2_.factor_ref), custom_call_target="tpu_custom_call" | custom-call | tf_op jit(solution)/shard_map/users_sum_again/pallas_call | solution.py:336
  224.2 6.9 %products_items.3 = f32[64,64,128]{2,1,0:T(8,128)} custom-call(s32[1]{0:T(128)} %bitcast.24.count_s, s32[512]{0:T(512)} %bitcast.36, s32[512]{0:T(512)} %bitcast.40, f32[64,64,128]{2,1,0:T(8,128)} %get-tuple-element.13.full_ref, bf16[512,128,128]{2,1,0:T(8,128)(2,1)} %bitcast.28), custom_call_target="tpu_custom_call" | custom-call | tf_op jit(solution)/shard_map/products_items/pallas_call | solution.py:66
  231.1 81.0 %items_reduce_last.1 = (f32[64,2048]{1,0:T(8,128)}, f32[64,256]{1,0:T(8,128)}) custom-call(f32[2,4,4,2,64,128]{5,4,3,2,1,0:T(8,128)} %bitcast.29, f32[64,64]{1,0:T(8,128)} %get-tuple-element.14.gram_ref, f32[2,128]{1,0:T(2,128)} %copy-done, f32[64,64]{1,0:T(8,128)} %get-tuple-element.12.refs_2_.factor_ref, f32[16,64,128]{2,1,0:T(8,128)} %get-tuple-element.15.users_ref), custom_call_target="tpu_custom_call" | custom-call | tf_op jit(solution)/shard_map/items_reduce_last/pallas_call | solution.py:336
  312.1 1.9 copy.15
  313.9 1.5 copy.16
Async XLA Ops:
  2.0 39.3 %copy-start = (f32[2,128]{1,0:T(2,128)}, f32[2,128]{1,0:T(2,128)S(1)}, u32[]{:S(2)}) copy-start(f32[2,128]{1,0:T(2,128)S(1)} %rsqrt_bitcast_fusion.1.scale_ref) | copy-start | bytes 3076

commit v2 on v1

v2 whole, which is shorter than its diff:
```python
import functools

import jax
import jax.numpy as jnp
from jax import lax
from jax.experimental import pallas as pl
from jax.experimental.pallas import tpu as pltpu
from jax.sharding import PartitionSpec as P

K = 64
H = K // 2
Q = K // 4
TILE = 128
UT = 64
IT = 64
CHUNK = 64
UNROLL = 64
NCH = 8
MESH = pl.DeviceIdType.MESH
F32 = jnp.float32
HIGHEST = lax.Precision.HIGHEST
VMEM_LIMIT = 56 * 1024 * 1024
VMEM = pl.BlockSpec(memory_space=pltpu.VMEM)


def tile_products(contract, count_s, from_s, to_s, full_ref, vals_ref, out_ref, split):
    g = pl.program_id(0)

    @pl.when(g == 0)
    def _():
        def prepare(j, carry):
            for q in range(4):
                x = full_ref[j * 4 + q]
                high = x.astype(jnp.bfloat16)
                split[j * 4 + q, :K] = high
                split[j * 4 + q, K:] = (x - high.astype(F32)).astype(jnp.bfloat16)
                out_ref[j * 4 + q] = jnp.zeros((K, TILE), F32)
            return carry

        lax.fori_loop(0, IT // 4, prepare, 0)

    count = count_s[0]
    live = jnp.clip(count - g * CHUNK, 0, CHUNK)

    def group(j, carry):
        base = j * UNROLL
        for q in range(UNROLL):
            both = lax.dot_general(
                split[from_s[g * CHUNK + base + q]],
                vals_ref[base + q],
                (((1,), (contract,)), ((), ())),
                preferred_element_type=F32,
            )
            to = to_s[g * CHUNK + base + q]
            out_ref[to] = out_ref[to] + jnp.where(base + q < live, both[:K] + both[K:], 0.0)
        return carry

    lax.fori_loop(0, (live + UNROLL - 1) // UNROLL, group, 0)


def products_call(contract, count, source, target, full, vals):
    slots = vals.shape[0]
    whole = pl.BlockSpec((UT, K, TILE), lambda g, n, a, b: (0, 0, 0))
    return pl.pallas_call(
        functools.partial(tile_products, contract),
        out_shape=jax.ShapeDtypeStruct((UT, K, TILE), F32),
        grid_spec=pltpu.PrefetchScalarGridSpec(
            num_scalar_prefetch=3,
            grid=(slots // CHUNK,),
            in_specs=[
                whole,
                pl.BlockSpec(
                    (CHUNK, TILE, TILE),
                    lambda g, n, a, b: (jnp.minimum(g, (n[0] - 1) // CHUNK), 0, 0),
                ),
            ],
            out_specs=whole,
            scratch_shapes=[pltpu.VMEM((UT, 2 * K, TILE), jnp.bfloat16)],
        ),
        compiler_params=pltpu.CompilerParams(vmem_limit_bytes=VMEM_LIMIT),
        name="products_users" if contract == 1 else "products_items",
    )(count, source, target, full, vals)


class Place:
    def __init__(self):
        users = lax.axis_index("users")
        items = lax.axis_index("items")
        self.xh, self.y, self.z = users // 16, (users // 4) % 4, users % 4
        self.xl, self.core = items // 2, items % 2

    def at(self, xh=None, y=None, z=None, xl=None, core=None):
        xh = self.xh if xh is None else xh
        y = self.y if y is None else y
        z = self.z if z is None else z
        xl = self.xl if xl is None else xl
        core = self.core if core is None else core
        return ((xh * 4 + y) * 4 + z, xl * 2 + core)

    def near(self):
        out = []
        for k in range(1, 8):
            j = (self.xh * 4 + self.xl * 2 + self.core + k) % 8
            out.append(self.at(xh=j // 4, xl=(j // 2) % 2, core=j % 2))
        return out

    def plane(self):
        out = []
        for k in range(1, 16):
            j = (self.y * 4 + self.z + k) % 16
            out.append(self.at(y=j // 4, z=j % 4))
        return out


def greet(devices):
    barrier = pltpu.get_barrier_semaphore()
    for device in devices:
        pl.semaphore_signal(barrier, inc=1, device_id=device, device_id_type=MESH)
    pl.semaphore_wait(barrier, len(devices))


class Sems:
    def __init__(self, send, recv):
        self.send, self.recv, self.used = send, recv, 0

    def copy(self, src, dst, device):
        k = self.used
        self.used += 1
        return pltpu.make_async_remote_copy(
            src_ref=src,
            dst_ref=dst,
            send_sem=self.send.at[k],
            recv_sem=self.recv.at[k],
            device_id=device,
            device_id_type=MESH,
        )


LOW, HIGH = slice(0, Q), slice(Q, H)


def rows(half, part=None):
    start = half * H + (Q if part is HIGH else 0)
    return pl.ds(start, H if part is None else Q)


class RingGather:
    def __init__(self, sems, slab, me, device):
        plus, minus, far = (me + 1) % 4, (me + 3) % 4, (me + 2) % 4
        to_plus, to_minus = device(plus), device(minus)
        self.own = [
            sems.copy(slab(me, None), slab(me, None), to_plus),
            sems.copy(slab(me, None), slab(me, None), to_minus),
        ]
        self.on = [
            sems.copy(slab(minus, LOW), slab(minus, LOW), to_plus),
            sems.copy(slab(plus, HIGH), slab(plus, HIGH), to_minus),
        ]
        del far

    def start(self):
        for copy in self.own:
            copy.start()

    def forward(self):
        for own, on in zip(self.own, self.on):
            own.wait_recv()
            on.start()

    def finish(self):
        for on in self.on:
            on.wait_recv()

    def drain(self):
        for copy in self.own + self.on:
            copy.wait_send()


class RingReduce:
    def __init__(self, sems, slab, me, device, first, second, sums):
        plus, minus, far = (me + 1) % 4, (me + 3) % 4, (me + 2) % 4
        to_plus, to_minus = device(plus), device(minus)
        self.slab, self.me, self.plus, self.minus = slab, me, plus, minus
        self.first, self.second, self.sums = first, second, sums
        self.far = [
            sems.copy(slab(far, LOW), first.at[0], to_plus),
            sems.copy(slab(far, HIGH), first.at[1], to_minus),
        ]
        self.plain = [
            sems.copy(slab(plus, HIGH), second.at[0, 1], to_plus),
            sems.copy(slab(minus, LOW), second.at[1, 0], to_minus),
        ]
        self.summed = [
            sems.copy(sums.at[0], second.at[0, 0], to_plus),
            sems.copy(sums.at[1], second.at[1, 1], to_minus),
        ]

    def start_far(self):
        for copy in self.far:
            copy.start()

    def start_plain(self):
        for copy in self.plain:
            copy.start()

    def forward(self):
        for k, (place, part) in enumerate(((self.plus, LOW), (self.minus, HIGH))):
            self.far[k].wait_recv()
            self.sums[k] = self.slab(place, part)[...] + self.first[k]
            self.summed[k].start()

    def finish(self, out_low, out_high):
        self.plain[1].wait_recv()
        self.summed[0].wait_recv()
        out_low[...] = self.slab(self.me, LOW)[...] + (self.second[0, 0] + self.second[1, 0])
        self.plain[0].wait_recv()
        self.summed[1].wait_recv()
        out_high[...] = self.slab(self.me, HIGH)[...] + (self.second[0, 1] + self.second[1, 1])

    def drain(self):
        for copy in self.far + self.plain + self.summed:
            copy.wait_send()


class GroupSum:
    def __init__(self, sems, buf, index, others):
        self.buf, self.index = buf, index
        self.copies = [sems.copy(buf.at[index], buf.at[index], d) for d in others]

    def start(self, value):
        self.buf[self.index] = value
        for copy in self.copies:
            copy.start()

    def finish(self):
        for copy in self.copies:
            copy.wait_recv()
        total = self.buf[0]
        for k in range(1, self.buf.shape[0]):
            total = total + self.buf[k]
        return total

    def drain(self):
        for copy in self.copies:
            copy.wait_send()


def near_sum(sems, place, buf):
    return GroupSum(sems, buf, place.xh * 4 + place.xl * 2 + place.core, place.near())


def plane_sum(sems, place, buf):
    return GroupSum(sems, buf, place.y * 4 + place.z, place.plane())


NEAR_BUF = pltpu.VMEM((8, K, K), F32)
PLANE_BUF = pltpu.VMEM((16, K, K), F32)


class Factor:
    def __init__(self, gram):
        self.row = lax.broadcasted_iota(jnp.int32, (K, 2 * K), 0)
        self.lane = lax.broadcasted_iota(jnp.int32, (K, 2 * K), 1)
        work = jnp.concatenate([gram, jnp.zeros((K, K), F32)], axis=1)
        self.work = work + jnp.where(self.lane == self.row + K, 1.0, 0.0)

    def columns(self, start, stop, step=8):
        work = self.work
        for j in range(start, stop, step):
            cols = [jnp.broadcast_to(work[:, k : k + 1], (K, 2 * K)) for k in range(j, j + step)]
            for s in range(step):
                k = j + s
                factor = jnp.where(self.row > k, cols[s] * (1.0 / cols[s][k : k + 1]), 0.0)
                for m in range(s + 1, step):
                    cols[m] = cols[m] - factor * cols[m][k : k + 1]
                work = work - factor * work[k : k + 1]
        self.work = work

    def inverse(self):
        pivots = jnp.sum(jnp.where(self.lane == self.row, self.work, 0.0), axis=1, keepdims=True)
        return self.work[:, K:] * lax.rsqrt(pivots)


def apply(left, right):
    return jnp.dot(left, right, precision=HIGHEST, preferred_element_type=F32)


def gram_of(tiles):
    total = jnp.zeros((K, K), F32)
    for x in tiles:
        total = total + lax.dot_general(
            x, x, (((1,), (1,)), ((), ())), precision=HIGHEST, preferred_element_type=F32
        )
    return total


class Spread:
    def __init__(self, sems, place, full):
        at_y, at_z = (lambda n: place.at(y=n)), (lambda n: place.at(z=n))
        y, z = place.y, place.z
        self.first = [
            RingGather(sems, lambda n, p: full.at[:, n, z, :, rows(0, p)], y, at_y),
            RingGather(sems, lambda n, p: full.at[:, y, n, :, rows(1, p)], z, at_z),
        ]
        order = lambda n: [n, (n + 3) % 4, (n + 1) % 4, (n + 2) % 4]
        self.second = [
            [RingGather(sems, lambda n, p, m=m: full.at[:, m, n, :, rows(0, p)], z, at_z) for m in order(y)],
            [RingGather(sems, lambda n, p, m=m: full.at[:, n, m, :, rows(1, p)], y, at_y) for m in order(z)],
        ]

    def start(self):
        for ring in self.first:
            ring.start()
        for rings in self.second:
            rings[0].start()

    def forward(self):
        for k in range(2):
            for ring, rings in zip(self.first, self.second):
                ring.own[k].wait_recv()
                ring.on[k].start()
                rings[1 + k].start()

    def turn(self):
        for rings in self.second:
            rings[0].forward()
        for ring, rings in zip(self.first, self.second):
            ring.finish()
            rings[3].start()

    def last(self):
        for k in (1, 2, 3):
            for rings in self.second:
                rings[k].forward()

    def finish(self):
        for k in range(4):
            for rings in self.second:
                rings[k].finish()

    def drain(self):
        for ring in self.first + self.second[0] + self.second[1]:
            ring.drain()


SPREAD_COPIES = 40


def across_x(sems, place, full):
    own = full.at[place.xh, place.y, place.z]
    return sems.copy(own, own, place.at(xh=1 - place.xh))


def gather_kernel(sent_ref, full, send, recv):
    place = Place()
    sems = Sems(send, recv)
    cross = across_x(sems, place, full)
    spread = Spread(sems, place, full)
    greet(
        [place.at(xh=1 - place.xh)]
        + [place.at(y=(place.y + k) % 4) for k in (1, 3)]
        + [place.at(z=(place.z + k) % 4) for k in (1, 3)]
    )
    full[place.xh, place.y, place.z] = sent_ref[...]
    cross.start()
    cross.wait_recv()
    spread.start()
    spread.forward()
    spread.turn()
    spread.last()
    spread.finish()
    cross.wait_send()
    spread.drain()


def remote_call(kernel, name, collective_id, out_shape, scratch_shapes, copies, *args):
    return pl.pallas_call(
        kernel,
        out_shape=out_shape,
        in_specs=[VMEM] * len(args),
        out_specs=jax.tree.map(lambda _: VMEM, out_shape),
        scratch_shapes=[
            *scratch_shapes,
            pltpu.SemaphoreType.DMA((copies,)),
            pltpu.SemaphoreType.DMA((copies,)),
        ],
        compiler_params=pltpu.CompilerParams(
            collective_id=collective_id, has_side_effects=True, vmem_limit_bytes=VMEM_LIMIT
        ),
        name=name,
    )(*args)


FULL = (2, 4, 4, 2, K, TILE)


def gather_call(sent):
    return remote_call(
        gather_kernel, "items_gather", 1, jax.ShapeDtypeStruct(FULL, F32), [], 1 + SPREAD_COPIES, sent
    )


def ring_bufs(lead):
    return [
        pltpu.VMEM((2, *lead, Q, TILE), F32),
        pltpu.VMEM((2, 2, *lead, Q, TILE), F32),
        pltpu.VMEM((2, *lead, Q, TILE), F32),
    ]


REDUCE_SCRATCH = (
    ring_bufs((2, 4, 2, 2))
    + ring_bufs((2, 2))
    + ring_bufs((2, 2))
    + [
        pltpu.VMEM((2, 2, 4, 2, H, TILE), F32),
        pltpu.VMEM((2, 2, K, TILE), F32),
        pltpu.VMEM((2, K, TILE), F32),
    ]
)
REDUCE_COPIES = 60 + 1


class Reduce:
    def __init__(self, sems, place, partial, bufs):
        a1, a2, a3, b1, b2, b3, c1, c2, c3, kept, mine, arrived = bufs
        at_y, at_z = (lambda n: place.at(y=n)), (lambda n: place.at(z=n))
        y, z = place.y, place.z
        self.place, self.mine, self.arrived = place, mine, arrived
        order = lambda n: [(n + 2) % 4, (n + 1) % 4, (n + 3) % 4, n]
        part = lambda p: slice(0, H) if p is None else p
        view = lambda ref, h, k: ref.at[:, h, k]
        view2 = lambda ref, h, k: ref.at[:, :, h, k]
        slab0 = lambda m: lambda n, p: partial.at[:, m, n, :, rows(0, p)]
        slab1 = lambda m: lambda n, p: partial.at[:, n, m, :, rows(1, p)]
        self.first = [
            [RingReduce(sems, slab0(m), z, at_z, view(a1, 0, k), view2(a2, 0, k), view(a3, 0, k))
             for k, m in enumerate(order(y))],
            [RingReduce(sems, slab1(m), y, at_y, view(a1, 1, k), view2(a2, 1, k), view(a3, 1, k))
             for k, m in enumerate(order(z))],
        ]
        self.outs = [
            [[kept.at[h, :, m, :, LOW], kept.at[h, :, m, :, HIGH]] for m in order(n)] for h, n in ((0, y), (1, z))
        ]
        self.second = [
            RingReduce(sems, lambda n, p: kept.at[0, :, n, :, part(p)], y, at_y, b1, b2, b3),
            RingReduce(sems, lambda n, p: kept.at[1, :, n, :, part(p)], z, at_z, c1, c2, c3),
        ]
        self.cross = sems.copy(mine.at[1 - place.xh], arrived, place.at(xh=1 - place.xh))

    def start(self):
        for k in range(4):
            for rings in self.first:
                rings[k].start_far()
        for k in range(4):
            for rings in self.first:
                rings[k].start_plain()

    def forward(self):
        for k in range(4):
            for rings in self.first:
                rings[k].forward()

    def turn(self):
        for rings, out, later in zip(self.first, self.outs, self.second):
            rings[0].finish(*out[0])
            later.start_far()

    def middle(self):
        for k in (1, 2):
            for rings, out in zip(self.first, self.outs):
                rings[k].finish(*out[k])
        for later in self.second:
            later.start_plain()
            later.forward()

    def last(self):
        for rings, out in zip(self.first, self.outs):
            rings[3].finish(*out[3])
        for half, later in enumerate(self.second):
            later.finish(self.mine.at[:, :, rows(half, LOW)], self.mine.at[:, :, rows(half, HIGH)])
        self.cross.start()

    def finish(self):
        self.cross.wait_recv()

    def total(self, t):
        return self.mine[self.place.xh, t] + self.arrived[t]

    def drain(self):
        for ring in self.first[0] + self.first[1] + self.second:
            ring.drain()
        self.cross.wait_send()


def reduced(reduce, near, plane_ref, user_total):
    near.start(plane_ref[...])
    reduce.start()
    reduce.forward()
    factor = Factor(near.finish() / user_total)
    factor.columns(0, K // 2)
    reduce.turn()
    reduce.middle()
    factor.columns(K // 2, K)
    inverse = factor.inverse()
    reduce.last()
    return inverse


def middle_kernel(user_total, partial, plane_ref, scale_ref, full, near_ref, *scratch):
    *bufs, near1, near2, send, recv = scratch
    place = Place()
    sems = Sems(send, recv)
    reduce = Reduce(sems, place, partial, bufs)
    gram1, gram2 = near_sum(sems, place, near1), near_sum(sems, place, near2)
    cross = across_x(sems, place, full)
    spread = Spread(sems, place, full)
    greet(place.near() + place.plane())

    inverse = reduced(reduce, gram1, plane_ref, user_total)
    reduce.finish()
    raw = [apply(inverse, scale_ref[t : t + 1] * reduce.total(t)) for t in range(2)]
    for t in range(2):
        full[place.xh, place.y, place.z, t] = scale_ref[t : t + 1] * raw[t]
    cross.start()
    gram2.start(gram_of(raw))
    cross.wait_recv()
    spread.start()
    spread.forward()
    spread.turn()
    spread.last()
    near_ref[...] = gram2.finish()
    spread.finish()
    cross.wait_send()
    for part in (reduce, spread, gram1, gram2):
        part.drain()


def middle_call(user_total, partial, plane, scale):
    return remote_call(
        functools.partial(middle_kernel, user_total),
        "items_reduce_gather",
        2,
        (jax.ShapeDtypeStruct(FULL, F32), jax.ShapeDtypeStruct((K, K), F32)),
        [*REDUCE_SCRATCH, NEAR_BUF, NEAR_BUF],
        REDUCE_COPIES + 14 + 1 + SPREAD_COPIES,
        partial,
        plane,
        scale,
    )


def last_kernel(
    user_total, item_total, partial, plane_ref, scale_ref, factor_ref, users_ref, user_out, item_out, *scratch
):
    *bufs, near1, near2, plane2, send, recv = scratch
    place = Place()
    sems = Sems(send, recv)
    reduce = Reduce(sems, place, partial, bufs)
    gram1, gram2 = near_sum(sems, place, near1), near_sum(sems, place, near2)
    gram2_plane = plane_sum(sems, place, plane2)
    greet(place.near() + place.plane())

    inverse = reduced(reduce, gram1, plane_ref, user_total)
    reduce.finish()
    raw = [apply(inverse, apply(factor_ref[...], scale_ref[t : t + 1] * reduce.total(t))) for t in range(2)]
    gram2.start(gram_of(raw))
    for t in range(8):
        user_out[:, t * TILE : (t + 1) * TILE] = apply(inverse, users_ref[t])
    gram2_plane.start(gram2.finish())
    for t in range(8, 16):
        user_out[:, t * TILE : (t + 1) * TILE] = apply(inverse, users_ref[t])
    factor = Factor(gram2_plane.finish() / item_total)
    factor.columns(0, K)
    inverse2 = factor.inverse()
    for t in range(2):
        item_out[:, t * TILE : (t + 1) * TILE] = apply(inverse2, raw[t])
    for part in (reduce, gram1, gram2, gram2_plane):
        part.drain()


def last_call(user_total, item_total, partial, plane, scale, factor, users):
    return remote_call(
        functools.partial(last_kernel, user_total, item_total),
        "items_reduce_last",
        3,
        (jax.ShapeDtypeStruct((K, 16 * TILE), F32), jax.ShapeDtypeStruct((K, 2 * TILE), F32)),
        [*REDUCE_SCRATCH, NEAR_BUF, NEAR_BUF, PLANE_BUF],
        REDUCE_COPIES + 14 + 15,
        partial,
        plane,
        scale,
        factor,
        users,
    )


def users_kernel(item_total, *refs):
    again = item_total is not None
    if again:
        partial, scale_ref, near_ref, full, raw_ref, plane_ref, factor_ref, *refs = refs
        item_plane, *refs = refs
    else:
        partial, scale_ref, full, raw_ref, plane_ref, *refs = refs
    from_core, from_chip, sums, user_plane, send, recv = refs
    place = Place()
    sems = Sems(send, recv)
    xl, core = place.xl, place.core
    size = 16 // NCH
    sibling = place.at(core=1 - core)
    partner = place.at(xl=1 - xl)

    def tiles(xq, cq, j):
        return pl.ds((xq * 2 + cq) * 16 + j * size, size)

    def to_core(xq, slot):
        return [
            sems.copy(partial.at[tiles(xq, 1 - core, j)], from_core.at[slot, j], sibling) for j in range(NCH)
        ]

    core_other, core_mine = to_core(1 - xl, 0), to_core(xl, 1)
    to_chip = [sems.copy(sums.at[j], from_chip.at[j], partner) for j in range(NCH)]
    mine = [full.at[tiles(xl, core, j)] for j in range(NCH)]
    theirs = [full.at[tiles(1 - xl, core, j)] for j in range(NCH)]
    done_chip = [sems.copy(mine[j], mine[j], partner) for j in range(NCH)]
    done_core = [sems.copy(mine[j], mine[j], sibling) for j in range(NCH)]
    passed = [sems.copy(theirs[j], theirs[j], sibling) for j in range(NCH)]
    gram = plane_sum(sems, place, user_plane)
    if again:
        item_gram = plane_sum(sems, place, item_plane)
    greet([sibling, partner] + place.plane())

    for copy in core_other + core_mine:
        copy.start()
    if again:
        item_gram.start(near_ref[...])
    for j in range(NCH):
        core_other[j].wait_recv()
        sums[j] = partial[tiles(1 - xl, core, j)] + from_core[0, j]
        to_chip[j].start()
    if again:
        factor = Factor(item_gram.finish() / item_total)
        factor.columns(0, K)
        factor_ref[...] = factor.inverse()
    for j in range(NCH):
        core_mine[j].wait_recv()
        to_chip[j].wait_recv()
        for t in range(size):
            row = j * size + t
            scale = scale_ref[row : row + 1]
            place_t = (xl * 2 + core) * 16 + row
            raw = scale * (partial[place_t] + (from_core[1, j, t] + from_chip[j, t]))
            full[place_t] = scale * raw
            raw_ref[row] = raw
        done_chip[j].start()
        done_core[j].start()
    if again:
        for t in range(16):
            raw_ref[t] = apply(factor_ref[...], raw_ref[t])
    gram.start(gram_of([raw_ref[t] for t in range(16)]))
    for j in range(NCH):
        done_chip[j].wait_recv()
        passed[j].start()
    for j in range(NCH):
        done_core[j].wait_recv()
        passed[j].wait_recv()
    plane_ref[...] = gram.finish()
    for copy in core_other + core_mine + to_chip + done_chip + done_core + passed:
        copy.wait_send()
    gram.drain()
    if again:
        item_gram.drain()


def users_call(partial, scale, near=None, item_total=None):
    size = 16 // NCH
    square = jax.ShapeDtypeStruct((K, K), F32)
    again = near is not None
    return remote_call(
        functools.partial(users_kernel, item_total),
        "users_sum_again" if again else "users_sum",
        5 if again else 4,
        (
            jax.ShapeDtypeStruct((UT, K, TILE), F32),
            jax.ShapeDtypeStruct((16, K, TILE), F32),
            *([square] * (2 if again else 1)),
        ),
        [
            *([PLANE_BUF] if again else []),
            pltpu.VMEM((2, NCH, size, K, TILE), F32),
            pltpu.VMEM((NCH, size, K, TILE), F32),
            pltpu.VMEM((NCH, size, K, TILE), F32),
            PLANE_BUF,
        ],
        7 * NCH + 30,
        partial,
        scale,
        *([near] if again else []),
    )


def body(tile_rows, tile_cols, tile_count, tile_vals, user_degree, item_degree, start_items):
    tile_row, tile_col, count = tile_rows[0, 0], tile_cols[0, 0], tile_count[0]
    vals = tile_vals[0, 0]
    user_scale = lax.rsqrt(user_degree.astype(F32)).reshape(16, TILE)
    item_scale = lax.rsqrt(item_degree.astype(F32)).reshape(2, TILE)
    user_total = 16 * TILE * lax.axis_size("users") * lax.axis_size("items")
    item_total = 2 * TILE * lax.axis_size("users") * lax.axis_size("items")
    sent = item_scale[:, None, :] * start_items.astype(F32).reshape(K, 2, TILE).transpose(1, 0, 2)

    full_items = gather_call(sent)
    partial = products_call(1, count, tile_col, tile_row, full_items.reshape(IT, K, TILE), vals)
    full_users, _, plane = users_call(partial, user_scale)
    partial = products_call(0, count, tile_row, tile_col, full_users, vals)
    full_items, near = middle_call(user_total, partial.reshape(FULL), plane, item_scale)
    partial = products_call(1, count, tile_col, tile_row, full_items.reshape(IT, K, TILE), vals)
    full_users, raw, plane, factor = users_call(partial, user_scale, near, item_total)
    partial = products_call(0, count, tile_row, tile_col, full_users, vals)
    return last_call(user_total, item_total, partial.reshape(FULL), plane, item_scale, factor, raw)


def solution(mesh):
    in_specs = (
        P("users", "items", None),
        P("users", "items", None),
        P("users", "items"),
        P("users", "items", None, None, None),
        P(("users", "items")),
        P(("items", "users")),
        P(None, ("items", "users")),
    )
    out_specs = (P(None, ("users", "items")), P(None, ("items", "users")))
    return jax.shard_map(body, mesh=mesh, in_specs=in_specs, out_specs=out_specs, check_vma=False)
```

time: 316 us -> 263 us (0.83)
  Pallas kernels: 307 us -> 253 us
    pallas_call x5, Pallas kernels: 278 us -> 192 us  [remote_call(): pl.pallas_call(kernel, out_shape=out_shape, in_specs=[VMEM] * len(args),...]
    pallas_call x4, Pallas kernels: 29 us -> 61.6 us  [products_call(): pl.pallas_call(functools.partial(tile_products, contract), out_shape=jax....]
where the time goes in v2:
time: 263 us; the launch traced here: 262 us
  Pallas kernels  253 us (96%)
  other arithmetic  3.38 us (1%)
  local copies, waits for them, and re-layouts  3.35 us (1%)
    pallas_call x5, Pallas kernels, remote_call(): pl.pallas_call(kernel, out_shape=out_shape, in_specs=[VMEM] * len(args),...  192 us
    pallas_call x4, Pallas kernels, products_call(): pl.pallas_call(functools.partial(tile_products, contract), out_shape=jax....  61.6 us

profile of v2, /device:TPU:1, one launch (start us, length us, event | category | flops | bytes accessed | tf_op | source)
XLA Modules:
  0.0 261.5 jit_solution(12337925787826091543)
XLA Ops:
  1.3 0.7 rsqrt_bitcast_fusion.1.scale_ref
  2.0 0.0 copy-start
  2.0 1.3 rsqrt_bitcast_fusion.refs_1_
  3.3 1.4 fusion.sent_ref
  4.7 26.7 %items_gather.1 = f32[2,4,4,2,64,128]{5,4,3,2,1,0:T(8,128)} custom-call(f32[2,64,128]{2,1,0:T(8,128)} %fusion.sent_ref), custom_call_target="tpu_custom_call" | custom-call | tf_op jit(solution)/shard_map/items_gather/pallas_call | solution.py:377
  31.3 17.2 %products_users.2.refs_0_ = f32[64,64,128]{2,1,0:T(8,128)} custom-call(s32[1]{0:T(128)} %bitcast.21.count_s, s32[512]{0:T(512)} %bitcast.37, s32[512]{0:T(512)} %bitcast.33, f32[64,64,128]{2,1,0:T(8,128)} %bitcast.31, bf16[512,128,128]{2,1,0:T(8,128)(2,1)} %bitcast.25), custom_call_target="tpu_custom_call" | custom-call | tf_op jit(solution)/shard_map/products_users/pallas_call | solution.py:64
  48.5 0.0 copy-done
  48.6 37.4 %users_sum.1 = (f32[64,64,128]{2,1,0:T(8,128)}, f32[16,64,128]{2,1,0:T(8,128)}, f32[64,64]{1,0:T(8,128)}) custom-call(f32[64,64,128]{2,1,0:T(8,128)} %products_users.2.refs_0_, f32[16,128]{1,0:T(8,128)} %rsqrt_bitcast_fusion.refs_1_), custom_call_target="tpu_custom_call" | custom-call | tf_op jit(solution)/shard_map/users_sum/pallas_call | solution.py:377
  85.9 13.5 %products_items.2 = f32[64,64,128]{2,1,0:T(8,128)} custom-call(s32[1]{0:T(128)} %bitcast.22.count_s, s32[512]{0:T(512)} %bitcast.34, s32[512]{0:T(512)} %bitcast.38, f32[64,64,128]{2,1,0:T(8,128)} %get-tuple-element.10.full_ref, bf16[512,128,128]{2,1,0:T(8,128)(2,1)} %bitcast.26), custom_call_target="tpu_custom_call" | custom-call | tf_op jit(solution)/shard_map/products_items/pallas_call | solution.py:64
  99.4 42.4 %items_reduce_gather.1 = (f32[2,4,4,2,64,128]{5,4,3,2,1,0:T(8,128)}, f32[64,64]{1,0:T(8,128)}) custom-call(f32[2,4,4,2,64,128]{5,4,3,2,1,0:T(8,128)} %bitcast.30, f32[64,64]{1,0:T(8,128)} %get-tuple-element.11.plane_ref, f32[2,128]{1,0:T(2,128)} %copy-done), custom_call_target="tpu_custom_call" | custom-call | tf_op jit(solution)/shard_map/items_reduce_gather/pallas_call | solution.py:377
  141.8 17.2 %products_users.3.refs_0_ = f32[64,64,128]{2,1,0:T(8,128)} custom-call(s32[1]{0:T(128)} %bitcast.23.count_s, s32[512]{0:T(512)} %bitcast.39, s32[512]{0:T(512)} %bitcast.35, f32[64,64,128]{2,1,0:T(8,128)} %bitcast.32, bf16[512,128,128]{2,1,0:T(8,128)(2,1)} %bitcast.27), custom_call_target="tpu_custom_call" | custom-call | tf_op jit(solution)/shard_map/products_users/pallas_call | solution.py:64
  159.1 42.3 %users_sum_again.1 = (f32[64,64,128]{2,1,0:T(8,128)}, f32[16,64,128]{2,1,0:T(8,128)}, f32[64,64]{1,0:T(8,128)}, f32[64,64]{1,0:T(8,128)}) custom-call(f32[64,64,128]{2,1,0:T(8,128)} %products_users.3.refs_0_, f32[16,128]{1,0:T(8,128)} %rsqrt_bitcast_fusion.refs_1_, f32[64,64]{1,0:T(8,128)} %get-tuple-element.13.refs_2_), custom_call_target="tpu_custom_call" | custom-call | tf_op jit(solution)/shard_map/users_sum_again/pallas_call | solution.py:377
  201.4 13.7 %products_items.3 = f32[64,64,128]{2,1,0:T(8,128)} custom-call(s32[1]{0:T(128)} %bitcast.24.count_s, s32[512]{0:T(512)} %bitcast.36, s32[512]{0:T(512)} %bitcast.40, f32[64,64,128]{2,1,0:T(8,128)} %get-tuple-element.14.full_ref, bf16[512,128,128]{2,1,0:T(8,128)(2,1)} %bitcast.28), custom_call_target="tpu_custom_call" | custom-call | tf_op jit(solution)/shard_map/products_items/pallas_call | solution.py:64
  215.1 43.1 %items_reduce_last.1 = (f32[64,2048]{1,0:T(8,128)}, f32[64,256]{1,0:T(8,128)}) custom-call(f32[2,4,4,2,64,128]{5,4,3,2,1,0:T(8,128)} %bitcast.29, f32[64,64]{1,0:T(8,128)} %get-tuple-element.15.plane_ref, f32[2,128]{1,0:T(2,128)} %copy-done, f32[64,64]{1,0:T(8,128)} %get-tuple-element.16.factor_ref, f32[16,64,128]{2,1,0:T(8,128)} %get-tuple-element.17.users_ref), custom_call_target="tpu_custom_call" | custom-call | tf_op jit(solution)/shard_map/items_reduce_last/pallas_call | solution.py:377
  258.2 1.9 copy.15
  260.0 1.5 copy.16
Async XLA Ops:
  2.0 46.6 %copy-start = (f32[2,128]{1,0:T(2,128)}, f32[2,128]{1,0:T(2,128)S(1)}, u32[]{:S(2)}) copy-start(f32[2,128]{1,0:T(2,128)S(1)} %rsqrt_bitcast_fusion.1.scale_ref) | copy-start | bytes 3076

commit v3 on v0

v3 whole, which is shorter than its diff:
```python
import functools

import jax
import jax.numpy as jnp
from jax import lax
from jax.experimental import pallas as pl
from jax.experimental.pallas import tpu as pltpu
from jax.sharding import PartitionSpec as P

K = 64
KH = K // 2
H = KH // 2
Q = KH // 4
TILE = 128
UT = 64
IT = 64
ITERS = 2
UNROLL = 64
LOADS = 4
NCH = 2
SIZE = 16 // NCH
MESH = pl.DeviceIdType.MESH
F32 = jnp.float32
HIGHEST = lax.Precision.HIGHEST
VMEM_LIMIT = 63 * 1024 * 1024
VMEM = pl.BlockSpec(memory_space=pltpu.VMEM)
SMEM = pl.BlockSpec(memory_space=pltpu.SMEM)


class Place:
    def __init__(self):
        users = lax.axis_index("users")
        items = lax.axis_index("items")
        self.xh, self.y, self.z = users // 16, (users // 4) % 4, users % 4
        self.xl, self.core = items // 2, items % 2

    def at(self, xh=None, y=None, z=None, xl=None, core=None):
        xh = self.xh if xh is None else xh
        y = self.y if y is None else y
        z = self.z if z is None else z
        xl = self.xl if xl is None else xl
        core = self.core if core is None else core
        return ((xh * 4 + y) * 4 + z, xl * 2 + core)

    def near(self):
        out = []
        for k in range(1, 8):
            j = (self.xh * 4 + self.xl * 2 + self.core + k) % 8
            out.append(self.at(xh=j // 4, xl=(j // 2) % 2, core=j % 2))
        return out

    def plane(self):
        out = []
        for k in range(1, 16):
            j = (self.y * 4 + self.z + k) % 16
            out.append(self.at(y=j // 4, z=j % 4))
        return out


def greet(devices):
    barrier = pltpu.get_barrier_semaphore()
    for device in devices:
        pl.semaphore_signal(barrier, inc=1, device_id=device, device_id_type=MESH)
    pl.semaphore_wait(barrier, len(devices))


class Sems:
    def __init__(self, send, recv):
        self.send, self.recv, self.used = send, recv, 0

    def copy(self, src, dst, device):
        k = self.used
        self.used += 1
        return pltpu.make_async_remote_copy(
            src_ref=src,
            dst_ref=dst,
            send_sem=self.send.at[k],
            recv_sem=self.recv.at[k],
            device_id=device,
            device_id_type=MESH,
        )


LOW, HIGH = slice(0, Q), slice(Q, H)


def rows(way, part=None):
    start = way * H + (Q if part is HIGH else 0)
    return pl.ds(start, H if part is None else Q)


class RingGather:
    def __init__(self, sems, slab, me, device):
        plus, minus, far = (me + 1) % 4, (me + 3) % 4, (me + 2) % 4
        to_plus, to_minus = device(plus), device(minus)
        self.own = [
            sems.copy(slab(me, None), slab(me, None), to_plus),
            sems.copy(slab(me, None), slab(me, None), to_minus),
        ]
        self.on = [
            sems.copy(slab(minus, LOW), slab(minus, LOW), to_plus),
            sems.copy(slab(plus, HIGH), slab(plus, HIGH), to_minus),
        ]
        del far

    def start(self):
        for copy in self.own:
            copy.start()

    def forward(self):
        for own, on in zip(self.own, self.on):
            own.wait_recv()
            on.start()

    def finish(self):
        for on in self.on:
            on.wait_recv()

    def drain(self):
        for copy in self.own + self.on:
            copy.wait_send()


class RingReduce:
    def __init__(self, sems, slab, me, device, first, second, sums):
        plus, minus, far = (me + 1) % 4, (me + 3) % 4, (me + 2) % 4
        to_plus, to_minus = device(plus), device(minus)
        self.slab, self.me, self.plus, self.minus = slab, me, plus, minus
        self.first, self.second, self.sums = first, second, sums
        self.far = [
            sems.copy(slab(far, LOW), first.at[0], to_plus),
            sems.copy(slab(far, HIGH), first.at[1], to_minus),
        ]
        self.plain = [
            sems.copy(slab(plus, HIGH), second.at[0, 1], to_plus),
            sems.copy(slab(minus, LOW), second.at[1, 0], to_minus),
        ]
        self.summed = [
            sems.copy(sums.at[0], second.at[0, 0], to_plus),
            sems.copy(sums.at[1], second.at[1, 1], to_minus),
        ]

    def start(self):
        for copy in self.far + self.plain:
            copy.start()

    def forward(self):
        for k, (place, part) in enumerate(((self.plus, LOW), (self.minus, HIGH))):
            self.far[k].wait_recv()
            self.sums[k] = self.slab(place, part)[...] + self.first[k]
            self.summed[k].start()

    def finish(self, out_low, out_high):
        self.plain[1].wait_recv()
        self.summed[0].wait_recv()
        out_low[...] = self.slab(self.me, LOW)[...] + (self.second[0, 0] + self.second[1, 0])
        self.plain[0].wait_recv()
        self.summed[1].wait_recv()
        out_high[...] = self.slab(self.me, HIGH)[...] + (self.second[0, 1] + self.second[1, 1])

    def drain(self):
        for copy in self.far + self.plain + self.summed:
            copy.wait_send()


class GroupSum:
    def __init__(self, sems, buf, index, others):
        self.buf, self.index = buf, index
        self.copies = [sems.copy(buf.at[index], buf.at[index], d) for d in others]

    def start(self, value):
        self.buf[self.index] = value
        for copy in self.copies:
            copy.start()

    def finish(self):
        for copy in self.copies:
            copy.wait_recv()
        total = self.buf[0]
        for k in range(1, self.buf.shape[0]):
            total = total + self.buf[k]
        return total

    def drain(self):
        for copy in self.copies:
            copy.wait_send()


def near_sum(sems, place, buf):
    return GroupSum(sems, buf, place.xh * 4 + place.xl * 2 + place.core, place.near())


def plane_sum(sems, place, buf):
    return GroupSum(sems, buf, place.y * 4 + place.z, place.plane())


class Factor:
    def __init__(self, gram):
        self.row = lax.broadcasted_iota(jnp.int32, (K, 2 * K), 0)
        self.lane = lax.broadcasted_iota(jnp.int32, (K, 2 * K), 1)
        work = jnp.concatenate([gram, jnp.zeros((K, K), F32)], axis=1)
        self.work = work + jnp.where(self.lane == self.row + K, 1.0, 0.0)

    def columns(self, start, stop, step=8):
        work = self.work
        for j in range(start, stop, step):
            cols = [jnp.broadcast_to(work[:, k : k + 1], (K, 2 * K)) for k in range(j, j + step)]
            for s in range(step):
                k = j + s
                factor = jnp.where(self.row > k, cols[s] * (1.0 / cols[s][k : k + 1]), 0.0)
                for m in range(s + 1, step):
                    cols[m] = cols[m] - factor * cols[m][k : k + 1]
                work = work - factor * work[k : k + 1]
        self.work = work

    def inverse(self):
        pivots = jnp.sum(jnp.where(self.lane == self.row, self.work, 0.0), axis=1, keepdims=True)
        return self.work[:, K:] * lax.rsqrt(pivots)


def apply(left, right):
    return jnp.dot(left, right, precision=HIGHEST, preferred_element_type=F32)


def gram_of(tiles):
    total = jnp.zeros((K, K), F32)
    for x in tiles:
        total = total + lax.dot_general(
            x, x, (((1,), (1,)), ((), ())), precision=HIGHEST, preferred_element_type=F32
        )
    return total


class Spread:
    def __init__(self, sems, place, full):
        at_y, at_z = (lambda n: place.at(y=n)), (lambda n: place.at(z=n))
        y, z = place.y, place.z
        self.first = [
            RingGather(sems, lambda n, p: full.at[:, n, z, :, rows(0, p)], y, at_y),
            RingGather(sems, lambda n, p: full.at[:, y, n, :, rows(1, p)], z, at_z),
        ]
        self.second = [
            RingGather(sems, lambda n, p: full.at[:, :, n, :, rows(0, p)], z, at_z),
            RingGather(sems, lambda n, p: full.at[:, n, :, :, rows(1, p)], y, at_y),
        ]

    def start(self):
        for ring in self.first:
            ring.start()

    def forward(self):
        for ring in self.first:
            ring.forward()

    def turn(self):
        for ring, later in zip(self.first, self.second):
            ring.finish()
            later.start()

    def last(self):
        for ring in self.second:
            ring.forward()

    def finish(self):
        for ring in self.second:
            ring.finish()

    def drain(self):
        for ring in self.first + self.second:
            ring.drain()


SPREAD_COPIES = 16


def ring_bufs(lead):
    return [
        pltpu.VMEM((2, *lead, Q, TILE), F32),
        pltpu.VMEM((2, 2, *lead, Q, TILE), F32),
        pltpu.VMEM((2, *lead, Q, TILE), F32),
    ]


def reduce_bufs():
    return (
        ring_bufs((2, 4, 2))
        + ring_bufs((2, 4, 2))
        + ring_bufs((2, 2))
        + ring_bufs((2, 2))
        + [
            pltpu.VMEM((2, 4, 2, H, TILE), F32),
            pltpu.VMEM((2, 4, 2, H, TILE), F32),
            pltpu.VMEM((2, 2, KH, TILE), F32),
            pltpu.VMEM((2, KH, TILE), F32),
        ]
    )


REDUCE_BUFS = 16
REDUCE_COPIES = 25


class Reduce:
    def __init__(self, sems, place, partial, bufs):
        at_y, at_z = (lambda n: place.at(y=n)), (lambda n: place.at(z=n))
        y, z = place.y, place.z
        way0, way1, mine, arrived = bufs[12:16]
        self.place, self.mine, self.arrived = place, mine, arrived
        part = lambda p: slice(0, H) if p is None else p
        self.first = [
            RingReduce(sems, lambda n, p: partial.at[:, :, n, :, rows(0, p)], z, at_z, *bufs[0:3]),
            RingReduce(sems, lambda n, p: partial.at[:, n, :, :, rows(1, p)], y, at_y, *bufs[3:6]),
        ]
        self.second = [
            RingReduce(sems, lambda n, p: way0.at[:, n, :, part(p)], y, at_y, *bufs[6:9]),
            RingReduce(sems, lambda n, p: way1.at[:, n, :, part(p)], z, at_z, *bufs[9:12]),
        ]
        self.outs = [[way.at[:, :, :, LOW], way.at[:, :, :, HIGH]] for way in (way0, way1)]
        self.cross = sems.copy(mine.at[1 - place.xh], arrived, place.at(xh=1 - place.xh))

    def start(self):
        for ring in self.first:
            ring.start()

    def forward(self):
        for ring in self.first:
            ring.forward()

    def turn(self):
        for ring, out, later in zip(self.first, self.outs, self.second):
            ring.finish(*out)
            later.start()

    def last(self):
        for ring in self.second:
            ring.forward()

    def across(self):
        for way, ring in enumerate(self.second):
            ring.finish(self.mine.at[:, :, rows(way, LOW)], self.mine.at[:, :, rows(way, HIGH)])
        self.cross.start()

    def finish(self):
        self.cross.wait_recv()

    def total(self, t):
        return self.mine[self.place.xh, t] + self.arrived[t]

    def drain(self):
        for ring in self.first + self.second:
            ring.drain()
        self.cross.wait_send()


class UserSum:
    def __init__(self, sems, place, half, partial, full, from_core, from_chip, sums):
        xl, core = place.xl, place.core
        sibling, partner = place.at(core=1 - core), place.at(xl=1 - xl)
        self.rows = slice(half * KH, (half + 1) * KH)
        self.place, self.partial, self.full = place, partial, full
        self.from_core, self.from_chip, self.sums = from_core, from_chip, sums
        tiles = self.tiles
        chunks = range(NCH)

        def to_core(xq, slot):
            return [sems.copy(partial.at[tiles(xq, 1 - core, j)], from_core.at[slot, j], sibling) for j in chunks]

        self.core_other, self.core_mine = to_core(1 - xl, 0), to_core(xl, 1)
        self.to_chip = [sems.copy(sums.at[j], from_chip.at[j], partner) for j in chunks]
        mine = [full.at[tiles(xl, core, j)] for j in chunks]
        theirs = [full.at[tiles(1 - xl, core, j)] for j in chunks]
        self.done_chip = [sems.copy(m, m, partner) for m in mine]
        self.done_core = [sems.copy(m, m, sibling) for m in mine]
        self.passed = [sems.copy(t, t, sibling) for t in theirs]

    def tiles(self, xq, cq, j):
        return pl.ds((xq * 2 + cq) * 16 + j * SIZE, SIZE)

    def start(self):
        for copy in self.core_other + self.core_mine:
            copy.start()

    def sum(self):
        place = self.place
        for j in range(NCH):
            self.core_other[j].wait_recv()
            self.sums[j] = self.partial[self.tiles(1 - place.xl, place.core, j)] + self.from_core[0, j]
            self.to_chip[j].start()

    def combine(self, j, scale_ref, raw_ref):
        place = self.place
        self.core_mine[j].wait_recv()
        self.to_chip[j].wait_recv()
        for t in range(SIZE):
            row = j * SIZE + t
            tile = (place.xl * 2 + place.core) * 16 + row
            scale = scale_ref[row : row + 1]
            raw = scale * (self.partial[tile] + (self.from_core[1, j, t] + self.from_chip[j, t]))
            self.full[tile] = scale * raw
            raw_ref[row, self.rows] = raw
        self.done_chip[j].start()
        self.done_core[j].start()

    def hand_on(self):
        for j in range(NCH):
            self.done_chip[j].wait_recv()
            self.passed[j].start()

    def finish(self):
        for j in range(NCH):
            self.done_core[j].wait_recv()
            self.passed[j].wait_recv()

    def drain(self):
        for copy in self.core_other + self.core_mine + self.to_chip + self.done_chip + self.done_core + self.passed:
            copy.wait_send()


USER_COPIES = 6 * NCH


def products(order_s, last_s, side, tiles, load, store, split, sums, steps):
    def prepare(j, carry):
        for q in range(4):
            x = load(j * 4 + q)
            high = x.astype(jnp.bfloat16)
            split[j * 4 + q, :KH] = high
            split[j * 4 + q, KH:] = (x - high.astype(F32)).astype(jnp.bfloat16)
        return carry

    lax.fori_loop(0, IT // 4, prepare, 0)

    def group(j, total):
        for q in range(UNROLL):
            p = j * UNROLL + q
            both = jnp.dot(
                split[order_s[side, 1, p]], tiles[order_s[side, 0, p]], preferred_element_type=F32
            )
            total = jnp.where(order_s[side, 2, p] == 1, 0.0, total) + (both[:KH] + both[KH:])
            sums[p] = total
        for at, step in steps.items():
            pl.when(j == at)(step)
        return total

    lax.fori_loop(0, sums.shape[0] // UNROLL, group, jnp.zeros((KH, TILE), F32))

    def collect(j, carry):
        for q in range(4):
            r = j * 4 + q
            store(r, jnp.where(last_s[side, 1, r] == 1, sums[last_s[side, 0, r]], 0.0))
        return carry

    lax.fori_loop(0, UT // 4, collect, 0)


def whole_kernel(user_total, item_total, order_s, last_s, sent_ref, user_scale, item_scale, vals_ref, *refs):
    user_out, item_out, vals, turned, split, sums, full_items, full_users, part_users, part_items, raw_users, *refs = refs
    from_core, from_chip, chip_sums, near1, near2, plane1, plane2, load_sem, *refs = refs
    send, recv = refs[-2:]
    place = Place()
    xh, y, z = place.xh, place.y, place.z
    sems = Sems(send, recv)
    own = full_items.at[:, xh, y, z]
    cross = sems.copy(own, own, place.at(xh=1 - xh))
    spread = [Spread(sems, place, full_items.at[h]) for h in range(2)]
    reduce = [
        Reduce(sems, place, part_items.at[h], refs[h * REDUCE_BUFS : (h + 1) * REDUCE_BUFS]) for h in range(2)
    ]
    user = [
        UserSum(sems, place, h, part_users.at[h], full_users.at[h], from_core.at[h], from_chip.at[h], chip_sums.at[h])
        for h in range(2)
    ]
    user_near, item_near = near_sum(sems, place, near1), near_sum(sems, place, near2)
    user_plane, item_plane = plane_sum(sems, place, plane1), plane_sum(sems, place, plane2)
    slots = vals.shape[0]
    portion = slots // LOADS
    loads = [
        pltpu.make_async_copy(
            vals_ref.at[pl.ds(k * portion, portion)], vals.at[pl.ds(k * portion, portion)], load_sem.at[k]
        )
        for k in range(LOADS)
    ]
    for load in loads:
        load.start()
    greet(place.near() + place.plane())

    def turn_tiles(k):
        loads[k].wait()

        def some(j, carry):
            for q in range(8):
                at = k * portion + j * 8 + q
                turned[at] = vals[at].T
            return carry

        lax.fori_loop(0, portion // 8, some, 0)

    def place_of(ref, half, tile):
        return ref.at[half, tile // 32, (tile // 8) % 4, (tile // 2) % 4, tile % 2]

    def to_users(half, steps):
        def store(r, value):
            part_users[half, r] = value

        products(
            order_s, last_s, 0, turned, lambda i: place_of(full_items, half, i)[...], store, split, sums, steps
        )

    def to_items(half, steps):
        def store(r, value):
            place_of(part_items, half, r)[...] = value

        products(order_s, last_s, 1, vals, lambda i: full_users[half, i], store, split, sums, steps)

    own[...] = sent_ref[...]
    item_factor = None
    for step in range(ITERS):
        cross.start()
        first = step == 0
        if first:
            turn_tiles(0)
        else:
            item_near.start(gram_of(raw_items))
        cross.wait_recv()
        spread[0].start()
        if first:
            turn_tiles(1)
        spread[0].forward()
        spread[1].start()
        if first:
            turn_tiles(2)
        spread[0].turn()
        spread[1].forward()
        if first:
            turn_tiles(3)
        spread[0].last()
        spread[1].turn()
        spread[0].finish()

        def second_half():
            spread[1].last()

        to_users(0, {2: second_half})
        user[0].start()
        spread[1].finish()
        if not first:
            item_plane.start(item_near.finish())
        to_users(1, {0: user[0].sum, 6: lambda: user[0].combine(0, user_scale, raw_users)})
        user[1].start()
        user[0].combine(1, user_scale, raw_users)
        user[1].sum()
        if not first:
            factor = Factor(item_plane.finish() / item_total)
            factor.columns(0, K)
            item_factor = factor.inverse()
        user[0].hand_on()
        user[0].finish()
        to_items(
            0,
            {
                3: lambda: user[1].combine(0, user_scale, raw_users),
                6: lambda: user[1].combine(1, user_scale, raw_users),
            },
        )
        cross.wait_send()
        for part in spread:
            part.drain()
        reduce[0].start()
        if not first:
            for t in range(16):
                raw_users[t] = apply(item_factor, raw_users[t])
        user_plane.start(gram_of([raw_users[t] for t in range(16)]))
        user[1].hand_on()
        user[1].finish()

        def gram_step():
            user_near.start(user_plane.finish())

        to_items(1, {1: reduce[0].forward, 3: gram_step, 5: reduce[0].turn})
        reduce[1].start()
        reduce[0].last()
        factor = Factor(user_near.finish() / user_total)
        factor.columns(0, K // 2)
        reduce[1].forward()
        reduce[0].across()
        factor.columns(K // 2, K)
        user_factor = factor.inverse()
        reduce[1].turn()
        reduce[1].last()
        if not first:
            for t in range(16):
                user_out[:, t * TILE : (t + 1) * TILE] = apply(user_factor, raw_users[t])
        reduce[1].across()
        reduce[0].finish()
        reduce[1].finish()
        raw_items = []
        for t in range(2):
            total = jnp.concatenate([reduce[0].total(t), reduce[1].total(t)], axis=0)
            raw = item_scale[t : t + 1] * total
            if not first:
                raw = apply(item_factor, raw)
            raw_items.append(apply(user_factor, raw))
        for part in (*user, *reduce, user_plane, user_near):
            part.drain()
        if first:
            for t in range(2):
                sent = item_scale[t : t + 1] * raw_items[t]
                for h in range(2):
                    full_items[h, xh, y, z, t] = sent[h * KH : (h + 1) * KH]
        else:
            item_plane.drain()
            item_near.drain()

    item_near.start(gram_of(raw_items))
    item_plane.start(item_near.finish())
    factor = Factor(item_plane.finish() / item_total)
    factor.columns(0, K)
    last_factor = factor.inverse()
    for t in range(2):
        item_out[:, t * TILE : (t + 1) * TILE] = apply(last_factor, raw_items[t])
    item_near.drain()
    item_plane.drain()


def whole_call(user_total, item_total, order, last, sent, user_scale, item_scale, vals):
    slots = vals.shape[0]
    copies = 1 + 2 * (SPREAD_COPIES + REDUCE_COPIES + USER_COPIES) + 44
    tiles = pltpu.VMEM((slots, TILE, TILE), jnp.bfloat16)
    full = (2, 2, 4, 4, 2, KH, TILE)
    scratch = [
        tiles,
        tiles,
        pltpu.VMEM((IT, 2 * KH, TILE), jnp.bfloat16),
        pltpu.VMEM((slots, KH, TILE), F32),
        pltpu.VMEM(full, F32),
        pltpu.VMEM((2, UT, KH, TILE), F32),
        pltpu.VMEM((2, UT, KH, TILE), F32),
        pltpu.VMEM(full, F32),
        pltpu.VMEM((16, K, TILE), F32),
        pltpu.VMEM((2, 2, NCH, SIZE, KH, TILE), F32),
        pltpu.VMEM((2, NCH, SIZE, KH, TILE), F32),
        pltpu.VMEM((2, NCH, SIZE, KH, TILE), F32),
        pltpu.VMEM((8, K, K), F32),
        pltpu.VMEM((8, K, K), F32),
        pltpu.VMEM((16, K, K), F32),
        pltpu.VMEM((16, K, K), F32),
        pltpu.SemaphoreType.DMA((LOADS,)),
        *reduce_bufs(),
        *reduce_bufs(),
        pltpu.SemaphoreType.DMA((copies,)),
        pltpu.SemaphoreType.DMA((copies,)),
    ]
    return pl.pallas_call(
        functools.partial(whole_kernel, user_total, item_total),
        out_shape=(
            jax.ShapeDtypeStruct((K, 16 * TILE), F32),
            jax.ShapeDtypeStruct((K, 2 * TILE), F32),
        ),
        in_specs=[SMEM, SMEM, VMEM, VMEM, VMEM, pl.BlockSpec(memory_space=pl.ANY)],
        out_specs=(VMEM, VMEM),
        scratch_shapes=scratch,
        compiler_params=pltpu.CompilerParams(
            collective_id=1, has_side_effects=True, vmem_limit_bytes=VMEM_LIMIT
        ),
        name="cocluster",
    )(order, last, sent, user_scale, item_scale, vals)


def slot_order(rows, cols, count):
    slots = rows.shape[0]
    at = jnp.arange(slots, dtype=jnp.int32)
    dead = jnp.where(at < count, 0, UT)
    target = jnp.stack([rows, cols]) + dead
    source = jnp.stack([cols, rows])
    code = (target * IT + source) * slots + at
    rank = jnp.sum((code[:, None, :] < code[:, :, None]).astype(jnp.int32), axis=2)
    ranked = jnp.sum(jnp.where(rank[:, None, :] == at[None, :, None], code[:, None, :], 0), axis=2)
    slot, source, target = ranked % slots, (ranked // slots) % IT, ranked // (slots * IT)
    before = jnp.concatenate([jnp.full((2, 1), -1, jnp.int32), target[:, :-1]], axis=1)
    order = jnp.stack([slot, source, (target != before).astype(jnp.int32)], axis=1)
    line = jnp.arange(UT, dtype=jnp.int32)[None, :, None]
    upto = jnp.sum((target[:, None, :] <= line).astype(jnp.int32), axis=2)
    has = jnp.sum((target[:, None, :] == line).astype(jnp.int32), axis=2)
    last = jnp.stack([jnp.maximum(upto - 1, 0), (has > 0).astype(jnp.int32)], axis=1)
    return order, last


def body(tile_rows, tile_cols, tile_count, tile_vals, user_degree, item_degree, start_items):
    user_scale = lax.rsqrt(user_degree.astype(F32)).reshape(16, TILE)
    item_scale = lax.rsqrt(item_degree.astype(F32)).reshape(2, TILE)
    user_total = 16 * TILE * lax.axis_size("users") * lax.axis_size("items")
    item_total = 2 * TILE * lax.axis_size("users") * lax.axis_size("items")
    start = start_items.astype(F32).reshape(2, KH, 2, TILE).transpose(0, 2, 1, 3)
    order, last = slot_order(tile_rows[0, 0], tile_cols[0, 0], tile_count[0, 0])
    return whole_call(
        user_total, item_total, order, last, item_scale[None, :, None, :] * start, user_scale, item_scale, tile_vals[0, 0]
    )


def solution(mesh):
    in_specs = (
        P("users", "items", None),
        P("users", "items", None),
        P("users", "items"),
        P("users", "items", None, None, None),
        P(("users", "items")),
        P(("items", "users")),
        P(None, ("items", "users")),
    )
    out_specs = (P(None, ("users", "items")), P(None, ("items", "users")))
    return jax.shard_map(body, mesh=mesh, in_specs=in_specs, out_specs=out_specs, check_vma=False)
```

time: 1350 us -> 218 us (0.16); the launches traced: 1330 us -> 218 us
  waiting for transfers between devices: 576 us -> 0 us
  blocking collectives: 307 us -> 0 us
  other arithmetic: 260 us -> 5.63 us
  Pallas kernels: 0 us -> 207 us
  matrix products: 133 us -> 0 us
  local copies, waits for them, and re-layouts: 42.5 us -> 4.15 us
  between operations: 15.6 us -> 1.33 us
    reduce_scatter x4 -> x0, waiting for transfers between devices: 384 us -> none  [the longest x2 327 us: body(): lax.psum_scatter(partial_items, 'users', scatter_dimension=1, tiled=True)]
    psum x4 -> x0, blocking collectives: 307 us -> none  [the longest x2 174 us: body(): item_gram = lax.psum(local_gram(item_raw), ('users', 'items'))]
    scatter-add x4 -> x0, other arithmetic: 207 us -> none  [the longest x2 104 us: item_partial(): summed = jnp.zeros((K, IT, TILE), jnp.float32).at[:, cols, :].add(product)]
    pallas_call x0 -> x1, Pallas kernels: none -> 207 us  [whole_call(): pl.pallas_call(functools.partial(whole_kernel, user_total, item_total), o...]
    all_gather x4 -> x0, waiting for transfers between devices: 192 us -> none  [the longest x2 139 us: gather_items(): return lax.all_gather(sent, 'users', axis=1, tiled=True)]
    dot_general x8 -> x0, matrix products: 125 us -> none  [the longest x2 74.6 us: user_partial(): jnp.einsum('ktc,trc->ktr', picked, values, precision=lax.Precision.HIGHES...]
    another operation x20 -> x3, other arithmetic: 48.3 us -> 1.29 us  [the longest x2 0.7 us: slot_order(): jnp.stack([slot, source, (target != before).astype(jnp.int32)], axis=1)]
    gather x4 -> x0, local copies, waits for them, and re-layouts: 27.9 us -> none  [the longest x2 13.9 us: user_partial(): picked = jnp.take(full_items.reshape(K, IT, TILE), cols, axis=1)]
  transfers between devices with their start and end apart: 8 -> 0, of which waited for: 8 -> 0; matrix products, arithmetic and copies ran while one was open for 0% -> 0% of each run, Pallas kernels for 0% -> 0%
where the time goes in v3:
time: 218 us
  Pallas kernels  207 us (95%)
  other arithmetic  5.63 us (3%)
  local copies, waits for them, and re-layouts  4.15 us (2%)
    pallas_call x1, Pallas kernels, whole_call(): pl.pallas_call(functools.partial(whole_kernel, user_total, item_total), o...  207 us

profile of v3, /device:TPU:1, one launch (start us, length us, event | category | flops | bytes accessed | tf_op | source)
XLA Modules:
  0.0 217.7 jit_solution(16809477798828923553)
XLA Ops:
  1.3 0.7 rsqrt_bitcast_fusion.1.item_scale
  2.0 0.0 copy-start
  2.0 0.8 fusion.5
  2.7 0.4 convert_reduce_fusion
  3.2 0.3 select_reduce_fusion
  3.5 0.2 convert_reduce_fusion.2
  3.7 0.6 pad_add_fusion.1.last_s
  4.3 0.1 compare_convert_fusion
  4.4 0.6 pad_add_fusion.order_s
  5.0 1.3 rsqrt_bitcast_fusion.user_scale
  6.3 0.8 reshape.275
  7.1 0.6 fusion.sent_ref
  7.8 0.0 copy-done
  7.8 206.5 %cocluster.1 = (f32[64,2048]{1,0:T(8,128)}, f32[64,256]{1,0:T(8,128)}) custom-call(s32[2,3,512]{2,1,0:T(4,128)} %pad_add_fusion.order_s, s32[2,2,64]{2,1,0:T(2,128)} %pad_add_fusion.1.last_s, f32[2,2,32,128]{3,2,1,0:T(8,128)} %fusion.sent_ref, f32[16,128]{1,0:T(8,128)} %rsqrt_bitcast_fusion.user_scale, f32[2,128]{1,0:T(2,128)} %copy-done, ...), custom_call_target="tpu_custom_call" | custom-call | tf_op jit(solution)/shard_map/cocluster/pallas_call | solution.py:653
  214.3 1.9 copy.27
  216.2 1.5 copy.28
  (6 shorter events, 0.1 us)
Async XLA Ops:
  2.0 5.8 %copy-start = (f32[2,128]{1,0:T(2,128)}, f32[2,128]{1,0:T(2,128)S(1)}, u32[]{:S(2)}) copy-start(f32[2,128]{1,0:T(2,128)S(1)} %rsqrt_bitcast_fusion.1.item_scale) | copy-start | bytes 3076

commit v4 on v3

--- a/solution.py
+++ b/solution.py
@@ -57,6 +57,23 @@
         return out
 
 
+def octet(place, along_y):
+    line = place.y if along_y else place.z
+    out = []
+    for k in range(1, 8):
+        j = (place.xh * 4 + line + k) % 8
+        out.append((j // 4, j % 4, place.at(xh=j // 4, y=j % 4) if along_y else place.at(xh=j // 4, z=j % 4)))
+    return out
+
+
+def corners(place):
+    out = []
+    for k in range(1, 4):
+        out.append(place.at(xh=1 - place.xh, y=(place.y + k) % 4))
+        out.append(place.at(xh=1 - place.xh, z=(place.z + k) % 4))
+    return out
+
+
 def greet(devices):
     barrier = pltpu.get_barrier_semaphore()
     for device in devices:
@@ -235,42 +252,41 @@
     def __init__(self, sems, place, full):
         at_y, at_z = (lambda n: place.at(y=n)), (lambda n: place.at(z=n))
         y, z = place.y, place.z
-        self.first = [
-            RingGather(sems, lambda n, p: full.at[:, n, z, :, rows(0, p)], y, at_y),
-            RingGather(sems, lambda n, p: full.at[:, y, n, :, rows(1, p)], z, at_z),
-        ]
-        self.second = [
+        self.direct = []
+        for way in range(2):
+            block = full.at[place.xh, y, z, :, rows(way)]
+            self.direct += [sems.copy(block, block, device) for _, _, device in octet(place, way == 0)]
+        self.rings = [
             RingGather(sems, lambda n, p: full.at[:, :, n, :, rows(0, p)], z, at_z),
             RingGather(sems, lambda n, p: full.at[:, n, :, :, rows(1, p)], y, at_y),
         ]
 
     def start(self):
-        for ring in self.first:
+        for copy in self.direct:
+            copy.start()
+
+    def turn(self):
+        for way, ring in enumerate(self.rings):
+            for copy in self.direct[way * 7 : way * 7 + 7]:
+                copy.wait_recv()
             ring.start()
 
-    def forward(self):
-        for ring in self.first:
+    def last(self):
+        for ring in self.rings:
             ring.forward()
 
-    def turn(self):
-        for ring, later in zip(self.first, self.second):
+    def finish(self):
+        for ring in self.rings:
             ring.finish()
-            later.start()
-
-    def last(self):
-        for ring in self.second:
-            ring.forward()
-
-    def finish(self):
-        for ring in self.second:
-            ring.finish()
 
     def drain(self):
-        for ring in self.first + self.second:
+        for copy in self.direct:
+            copy.wait_send()
+        for ring in self.rings:
             ring.drain()
 
 
-SPREAD_COPIES = 16
+SPREAD_COPIES = 22
 
 
 def ring_bufs(lead):
@@ -285,71 +301,62 @@
     return (
         ring_bufs((2, 4, 2))
         + ring_bufs((2, 4, 2))
-        + ring_bufs((2, 2))
-        + ring_bufs((2, 2))
-        + [
-            pltpu.VMEM((2, 4, 2, H, TILE), F32),
-            pltpu.VMEM((2, 4, 2, H, TILE), F32),
-            pltpu.VMEM((2, 2, KH, TILE), F32),
-            pltpu.VMEM((2, KH, TILE), F32),
-        ]
+        + [pltpu.VMEM((2, 2, 4, 2, H, TILE), F32), pltpu.VMEM((2, 7, 2, H, TILE), F32)]
     )
 
 
-REDUCE_BUFS = 16
-REDUCE_COPIES = 25
+REDUCE_BUFS = 8
+REDUCE_COPIES = 26
 
 
 class Reduce:
     def __init__(self, sems, place, partial, bufs):
         at_y, at_z = (lambda n: place.at(y=n)), (lambda n: place.at(z=n))
         y, z = place.y, place.z
-        way0, way1, mine, arrived = bufs[12:16]
-        self.place, self.mine, self.arrived = place, mine, arrived
-        part = lambda p: slice(0, H) if p is None else p
-        self.first = [
+        self.ways, self.arrived = bufs[6:8]
+        self.place = place
+        self.rings = [
             RingReduce(sems, lambda n, p: partial.at[:, :, n, :, rows(0, p)], z, at_z, *bufs[0:3]),
             RingReduce(sems, lambda n, p: partial.at[:, n, :, :, rows(1, p)], y, at_y, *bufs[3:6]),
         ]
-        self.second = [
-            RingReduce(sems, lambda n, p: way0.at[:, n, :, part(p)], y, at_y, *bufs[6:9]),
-            RingReduce(sems, lambda n, p: way1.at[:, n, :, part(p)], z, at_z, *bufs[9:12]),
+        self.direct = [
+            [
+                sems.copy(self.ways.at[way, xh, line], self.arrived.at[way, k], device)
+                for k, (xh, line, device) in enumerate(octet(place, way == 0))
+            ]
+            for way in range(2)
         ]
-        self.outs = [[way.at[:, :, :, LOW], way.at[:, :, :, HIGH]] for way in (way0, way1)]
-        self.cross = sems.copy(mine.at[1 - place.xh], arrived, place.at(xh=1 - place.xh))
 
     def start(self):
-        for ring in self.first:
+        for ring in self.rings:
             ring.start()
 
     def forward(self):
-        for ring in self.first:
+        for ring in self.rings:
             ring.forward()
 
     def turn(self):
-        for ring, out, later in zip(self.first, self.outs, self.second):
-            ring.finish(*out)
-            later.start()
-
-    def last(self):
-        for ring in self.second:
-            ring.forward()
-
-    def across(self):
-        for way, ring in enumerate(self.second):
-            ring.finish(self.mine.at[:, :, rows(way, LOW)], self.mine.at[:, :, rows(way, HIGH)])
-        self.cross.start()
+        for way, ring in enumerate(self.rings):
+            ring.finish(self.ways.at[way, :, :, :, LOW], self.ways.at[way, :, :, :, HIGH])
+            for copy in self.direct[way]:
+                copy.start()
 
     def finish(self):
-        self.cross.wait_recv()
-
-    def total(self, t):
-        return self.mine[self.place.xh, t] + self.arrived[t]
+        place = self.place
+        sums = []
+        for way, line in enumerate((place.y, place.z)):
+            total = self.ways[way, place.xh, line]
+            for k, copy in enumerate(self.direct[way]):
+                copy.wait_recv()
+                total = total + self.arrived[way, k]
+            sums.append(total)
+        return [jnp.concatenate([sums[0][t], sums[1][t]], axis=0) for t in range(2)]
 
     def drain(self):
-        for ring in self.first + self.second:
+        for ring in self.rings:
             ring.drain()
-        self.cross.wait_send()
+        for copy in self.direct[0] + self.direct[1]:
+            copy.wait_send()
 
 
 class UserSum:
@@ -453,15 +460,13 @@
     lax.fori_loop(0, UT // 4, collect, 0)
 
 
-def whole_kernel(user_total, item_total, order_s, last_s, sent_ref, user_scale, item_scale, vals_ref, *refs):
+def whole_kernel(user_total, item_total, order_s, last_s, start_ref, user_degree, item_degree, vals_ref, *refs):
     user_out, item_out, vals, turned, split, sums, full_items, full_users, part_users, part_items, raw_users, *refs = refs
-    from_core, from_chip, chip_sums, near1, near2, plane1, plane2, load_sem, *refs = refs
+    from_core, from_chip, chip_sums, near1, near2, plane1, plane2, user_scale, load_sem, *refs = refs
     send, recv = refs[-2:]
     place = Place()
     xh, y, z = place.xh, place.y, place.z
     sems = Sems(send, recv)
-    own = full_items.at[:, xh, y, z]
-    cross = sems.copy(own, own, place.at(xh=1 - xh))
     spread = [Spread(sems, place, full_items.at[h]) for h in range(2)]
     reduce = [
         Reduce(sems, place, part_items.at[h], refs[h * REDUCE_BUFS : (h + 1) * REDUCE_BUFS]) for h in range(2)
@@ -482,7 +487,7 @@
     ]
     for load in loads:
         load.start()
-    greet(place.near() + place.plane())
+    greet(place.near() + place.plane() + corners(place))
 
     def turn_tiles(k):
         loads[k].wait()
@@ -512,35 +517,26 @@
 
         products(order_s, last_s, 1, vals, lambda i: full_users[half, i], store, split, sums, steps)
 
-    own[...] = sent_ref[...]
+    item_scale = lax.rsqrt(item_degree[...].astype(F32))
+    for h in range(2):
+        for t in range(2):
+            start = start_ref[h * KH : (h + 1) * KH, t * TILE : (t + 1) * TILE].astype(F32)
+            full_items[h, xh, y, z, t] = item_scale[t : t + 1] * start
+        spread[h].start()
+    user_scale[...] = lax.rsqrt(user_degree[...].astype(F32))
+    turn_tiles(0)
+    spread[0].turn()
+    turn_tiles(1)
+    spread[1].turn()
+    turn_tiles(2)
+    spread[0].last()
+    turn_tiles(3)
+    spread[0].finish()
     item_factor = None
     for step in range(ITERS):
-        cross.start()
         first = step == 0
-        if first:
-            turn_tiles(0)
-        else:
-            item_near.start(gram_of(raw_items))
-        cross.wait_recv()
-        spread[0].start()
-        if first:
-            turn_tiles(1)
-        spread[0].forward()
-        spread[1].start()
-        if first:
-            turn_tiles(2)
-        spread[0].turn()
-        spread[1].forward()
-        if first:
-            turn_tiles(3)
-        spread[0].last()
-        spread[1].turn()
-        spread[0].finish()
-
-        def second_half():
-            spread[1].last()
-
-        to_users(0, {2: second_half})
+
+        to_users(0, {3: spread[1].last} if first else {1: spread[1].turn, 5: spread[1].last})
         user[0].start()
         spread[1].finish()
         if not first:
@@ -554,15 +550,9 @@
             factor.columns(0, K)
             item_factor = factor.inverse()
         user[0].hand_on()
+        user[1].combine(0, user_scale, raw_users)
         user[0].finish()
-        to_items(
-            0,
-            {
-                3: lambda: user[1].combine(0, user_scale, raw_users),
-                6: lambda: user[1].combine(1, user_scale, raw_users),
-            },
-        )
-        cross.wait_send()
+        to_items(0, {0: lambda: user[1].combine(1, user_scale, raw_users), 7: user[1].hand_on})
         for part in spread:
             part.drain()
         reduce[0].start()
@@ -570,43 +560,49 @@
             for t in range(16):
                 raw_users[t] = apply(item_factor, raw_users[t])
         user_plane.start(gram_of([raw_users[t] for t in range(16)]))
-        user[1].hand_on()
         user[1].finish()
 
         def gram_step():
             user_near.start(user_plane.finish())
 
-        to_items(1, {1: reduce[0].forward, 3: gram_step, 5: reduce[0].turn})
+        to_items(1, {2: reduce[0].forward, 3: gram_step, 6: reduce[0].turn})
         reduce[1].start()
-        reduce[0].last()
         factor = Factor(user_near.finish() / user_total)
-        factor.columns(0, K // 2)
+        factor.columns(0, KH)
+        totals = [reduce[0].finish()]
+        if first:
+            top = factor.inverse()[:KH, :KH]
+            raw_top = [apply(top, item_scale[t : t + 1] * totals[0][t]) for t in range(2)]
+            for t in range(2):
+                full_items[0, xh, y, z, t] = item_scale[t : t + 1] * raw_top[t]
+            spread[0].start()
         reduce[1].forward()
-        reduce[0].across()
-        factor.columns(K // 2, K)
+        factor.columns(KH, K)
         user_factor = factor.inverse()
         reduce[1].turn()
-        reduce[1].last()
-        if not first:
+        if first:
+            spread[0].turn()
+        else:
             for t in range(16):
                 user_out[:, t * TILE : (t + 1) * TILE] = apply(user_factor, raw_users[t])
-        reduce[1].across()
-        reduce[0].finish()
-        reduce[1].finish()
+        totals.append(reduce[1].finish())
         raw_items = []
         for t in range(2):
-            total = jnp.concatenate([reduce[0].total(t), reduce[1].total(t)], axis=0)
-            raw = item_scale[t : t + 1] * total
-            if not first:
-                raw = apply(item_factor, raw)
-            raw_items.append(apply(user_factor, raw))
+            raw = item_scale[t : t + 1] * jnp.concatenate([totals[0][t], totals[1][t]], axis=0)
+            if first:
+                low = apply(user_factor[KH:], raw)
+                full_items[1, xh, y, z, t] = item_scale[t : t + 1] * low
+                raw_items.append(jnp.concatenate([raw_top[t], low], axis=0))
+            else:
+                raw_items.append(apply(user_factor, apply(item_factor, raw)))
+        if first:
+            spread[1].start()
+            item_near.start(gram_of(raw_items))
         for part in (*user, *reduce, user_plane, user_near):
             part.drain()
         if first:
-            for t in range(2):
-                sent = item_scale[t : t + 1] * raw_items[t]
-                for h in range(2):
-                    full_items[h, xh, y, z, t] = sent[h * KH : (h + 1) * KH]
+            spread[0].last()
+            spread[0].finish()
         else:
             item_plane.drain()
             item_near.drain()
@@ -622,9 +618,9 @@
     item_plane.drain()
 
 
-def whole_call(user_total, item_total, order, last, sent, user_scale, item_scale, vals):
+def whole_call(user_total, item_total, order, last, start, user_degree, item_degree, vals):
     slots = vals.shape[0]
-    copies = 1 + 2 * (SPREAD_COPIES + REDUCE_COPIES + USER_COPIES) + 44
+    copies = 2 * (SPREAD_COPIES + REDUCE_COPIES + USER_COPIES) + 44
     tiles = pltpu.VMEM((slots, TILE, TILE), jnp.bfloat16)
     full = (2, 2, 4, 4, 2, KH, TILE)
     scratch = [
@@ -644,6 +640,7 @@
         pltpu.VMEM((8, K, K), F32),
         pltpu.VMEM((16, K, K), F32),
         pltpu.VMEM((16, K, K), F32),
+        pltpu.VMEM((16, TILE), F32),
         pltpu.SemaphoreType.DMA((LOADS,)),
         *reduce_bufs(),
         *reduce_bufs(),
@@ -663,7 +660,7 @@
             collective_id=1, has_side_effects=True, vmem_limit_bytes=VMEM_LIMIT
         ),
         name="cocluster",
-    )(order, last, sent, user_scale, item_scale, vals)
+    )(order, last, start, user_degree, item_degree, vals)
 
 
 def slot_order(rows, cols, count):
@@ -686,15 +683,11 @@
 
 
 def body(tile_rows, tile_cols, tile_count, tile_vals, user_degree, item_degree, start_items):
-    user_scale = lax.rsqrt(user_degree.astype(F32)).reshape(16, TILE)
-    item_scale = lax.rsqrt(item_degree.astype(F32)).reshape(2, TILE)
     user_total = 16 * TILE * lax.axis_size("users") * lax.axis_size("items")
     item_total = 2 * TILE * lax.axis_size("users") * lax.axis_size("items")
-    start = start_items.astype(F32).reshape(2, KH, 2, TILE).transpose(0, 2, 1, 3)
     order, last = slot_order(tile_rows[0, 0], tile_cols[0, 0], tile_count[0, 0])
-    return whole_call(
-        user_total, item_total, order, last, item_scale[None, :, None, :] * start, user_scale, item_scale, tile_vals[0, 0]
-    )
+    degrees = user_degree.reshape(16, TILE), item_degree.reshape(2, TILE)
+    return whole_call(user_total, item_total, order, last, start_items, *degrees, tile_vals[0, 0])
 
 
 def solution(mesh):

time: 218 us -> 197 us (0.904)
  Pallas kernels: 207 us -> 189 us
  other arithmetic: 5.63 us -> 3 us
    pallas_call x1, Pallas kernels: 207 us -> 189 us  [whole_call(): pl.pallas_call(functools.partial(whole_kernel, user_total, item_total), o...]
where the time goes in v4:
time: 197 us
  Pallas kernels  189 us (96%)
  local copies, waits for them, and re-layouts  3.35 us (2%)
  other arithmetic  3 us (2%)
    pallas_call x1, Pallas kernels, whole_call(): pl.pallas_call(functools.partial(whole_kernel, user_total, item_total), o...  189 us

profile of v4, /device:TPU:1, one launch (start us, length us, event | category | flops | bytes accessed | tf_op | source)
XLA Modules:
  0.0 196.9 jit_solution(2680372194406298770)
XLA Ops:
  1.3 0.8 fusion.4
  2.1 0.4 convert_reduce_fusion
  2.5 0.3 select_reduce_fusion
  2.8 0.2 convert_reduce_fusion.2
  3.0 0.6 pad_add_fusion.1.last_s
  3.6 0.1 compare_convert_fusion
  3.7 0.6 pad_add_fusion.order_s
  4.3 189.3 %cocluster.1 = (f32[64,2048]{1,0:T(8,128)}, f32[64,256]{1,0:T(8,128)}) custom-call(s32[2,3,512]{2,1,0:T(4,128)} %pad_add_fusion.order_s, s32[2,2,64]{2,1,0:T(2,128)} %pad_add_fusion.1.last_s, bf16[64,256]{1,0:T(8,128)(2,1)} %start_ref.1, s32[16,128]{1,0:T(8,128)} %bitcast.16, s32[2,128]{1,0:T(2,128)} %bitcast.21, bf16[512,128,128]{2,1,0:T(8,128)(2,1)} %bitcast.14), custom_call_target="tpu_custom_call" | custom-call | tf_op jit(solution)/shard_map/cocluster/pallas_call | solution.py:650
  193.6 1.9 copy.18
  195.5 1.5 copy.19
  (6 shorter events, 0.1 us)

commit v5 on v4

--- a/solution.py
+++ b/solution.py
@@ -436,20 +436,21 @@
         return carry
 
     lax.fori_loop(0, IT // 4, prepare, 0)
+    split[IT] = jnp.zeros((2 * KH, TILE), jnp.bfloat16)
 
     def group(j, total):
-        for q in range(UNROLL):
-            p = j * UNROLL + q
-            both = jnp.dot(
-                split[order_s[side, 1, p]], tiles[order_s[side, 0, p]], preferred_element_type=F32
-            )
+        for q in range(UNROLL // 2):
+            p = j * UNROLL + 2 * q
+            panel = jnp.concatenate([split[order_s[side, 1, p]], split[order_s[side, 1, p + 1]]], axis=1)
+            pair = jnp.concatenate([tiles[order_s[side, 0, p]], tiles[order_s[side, 0, p + 1]]], axis=0)
+            both = jnp.dot(panel, pair, preferred_element_type=F32)
             total = jnp.where(order_s[side, 2, p] == 1, 0.0, total) + (both[:KH] + both[KH:])
-            sums[p] = total
+            sums[j * (UNROLL // 2) + q] = total
         for at, step in steps.items():
             pl.when(j == at)(step)
         return total
 
-    lax.fori_loop(0, sums.shape[0] // UNROLL, group, jnp.zeros((KH, TILE), F32))
+    lax.fori_loop(0, 2 * sums.shape[0] // UNROLL, group, jnp.zeros((KH, TILE), F32))
 
     def collect(j, carry):
         for q in range(4):
@@ -552,20 +553,25 @@
         user[0].hand_on()
         user[1].combine(0, user_scale, raw_users)
         user[0].finish()
-        to_items(0, {0: lambda: user[1].combine(1, user_scale, raw_users), 7: user[1].hand_on})
+
+        def users_gram():
+            if not first:
+                for t in range(16):
+                    raw_users[t] = apply(item_factor, raw_users[t])
+            user_plane.start(gram_of([raw_users[t] for t in range(16)]))
+
+        to_items(
+            0, {0: lambda: user[1].combine(1, user_scale, raw_users), 4: users_gram, 7: user[1].hand_on}
+        )
         for part in spread:
             part.drain()
         reduce[0].start()
-        if not first:
-            for t in range(16):
-                raw_users[t] = apply(item_factor, raw_users[t])
-        user_plane.start(gram_of([raw_users[t] for t in range(16)]))
         user[1].finish()
 
         def gram_step():
             user_near.start(user_plane.finish())
 
-        to_items(1, {2: reduce[0].forward, 3: gram_step, 6: reduce[0].turn})
+        to_items(1, {0: gram_step, 2: reduce[0].forward, 6: reduce[0].turn})
         reduce[1].start()
         factor = Factor(user_near.finish() / user_total)
         factor.columns(0, KH)
@@ -626,8 +632,8 @@
     scratch = [
         tiles,
         tiles,
-        pltpu.VMEM((IT, 2 * KH, TILE), jnp.bfloat16),
-        pltpu.VMEM((slots, KH, TILE), F32),
+        pltpu.VMEM((IT + 1, 2 * KH, TILE), jnp.bfloat16),
+        pltpu.VMEM(((slots + UT) // 2, KH, TILE), F32),
         pltpu.VMEM(full, F32),
         pltpu.VMEM((2, UT, KH, TILE), F32),
         pltpu.VMEM((2, UT, KH, TILE), F32),
@@ -671,14 +677,20 @@
     source = jnp.stack([cols, rows])
     code = (target * IT + source) * slots + at
     rank = jnp.sum((code[:, None, :] < code[:, :, None]).astype(jnp.int32), axis=2)
-    ranked = jnp.sum(jnp.where(rank[:, None, :] == at[None, :, None], code[:, None, :], 0), axis=2)
-    slot, source, target = ranked % slots, (ranked // slots) % IT, ranked // (slots * IT)
-    before = jnp.concatenate([jnp.full((2, 1), -1, jnp.int32), target[:, :-1]], axis=1)
+    line = jnp.arange(UT, dtype=jnp.int32)
+    has = jnp.sum((target[:, None, :] == line[None, :, None]).astype(jnp.int32), axis=2)
+    odd = has % 2
+    moved = jnp.sum(jnp.where(line[None, :, None] < target[:, None, :], odd[:, :, None], 0), axis=1)
+    place = jnp.arange(slots + UT, dtype=jnp.int32)[None, :, None]
+    ranked = jnp.sum(jnp.where((rank + moved)[:, None, :] == place, code[:, None, :] + 1, 0), axis=2) - 1
+    none = ranked < 0
+    slot = jnp.where(none, 0, ranked % slots)
+    source = jnp.where(none, IT, (ranked // slots) % IT)
+    target = ranked // (slots * IT)
+    before = jnp.concatenate([jnp.full((2, 2), -1, jnp.int32), target[:, :-2]], axis=1)
     order = jnp.stack([slot, source, (target != before).astype(jnp.int32)], axis=1)
-    line = jnp.arange(UT, dtype=jnp.int32)[None, :, None]
-    upto = jnp.sum((target[:, None, :] <= line).astype(jnp.int32), axis=2)
-    has = jnp.sum((target[:, None, :] == line).astype(jnp.int32), axis=2)
-    last = jnp.stack([jnp.maximum(upto - 1, 0), (has > 0).astype(jnp.int32)], axis=1)
+    upto = jnp.sum(jnp.where(line[None, None, :] <= line[None, :, None], (has + odd)[:, None, :], 0), axis=2)
+    last = jnp.stack([jnp.maximum(upto // 2 - 1, 0), (has > 0).astype(jnp.int32)], axis=1)
     return order, last
 
 

time: 197 us -> 191 us (0.970)
  Pallas kernels: 189 us -> 183 us
    pallas_call x1, Pallas kernels: 189 us -> 183 us  [whole_call(): pl.pallas_call(functools.partial(whole_kernel, user_total, item_total), o...]
where the time goes in v5:
time: 191 us
  Pallas kernels  183 us (96%)
  local copies, waits for them, and re-layouts  3.36 us (2%)
  other arithmetic  3.28 us (2%)
    pallas_call x1, Pallas kernels, whole_call(): pl.pallas_call(functools.partial(whole_kernel, user_total, item_total), o...  183 us

profile of v5, /device:TPU:1, one launch (start us, length us, event | category | flops | bytes accessed | tf_op | source)
XLA Modules:
  0.0 190.6 jit_solution(13198305185742765808)
XLA Ops:
  1.3 0.8 broadcast_add_fusion.1
  2.1 0.1 convert_reduce_fusion.1
  2.2 0.1 select_reduce_fusion.2
  2.4 0.6 pad_add_fusion.1.last_s
  3.0 0.1 select_reduce_fusion.1
  3.1 0.4 convert_reduce_fusion
  3.5 0.4 select_reduce_fusion
  3.9 0.1 compare_convert_fusion
  4.0 0.6 pad_add_fusion.order_s
  4.7 182.6 %cocluster.1 = (f32[64,2048]{1,0:T(8,128)}, f32[64,256]{1,0:T(8,128)}) custom-call(s32[2,3,576]{2,1,0:T(4,128)} %pad_add_fusion.order_s, s32[2,2,64]{2,1,0:T(2,128)} %pad_add_fusion.1.last_s, bf16[64,256]{1,0:T(8,128)(2,1)} %start_ref.1, s32[16,128]{1,0:T(8,128)} %bitcast.32, s32[2,128]{1,0:T(2,128)} %bitcast.37, bf16[512,128,128]{2,1,0:T(8,128)(2,1)} %bitcast.30), custom_call_target="tpu_custom_call" | custom-call | tf_op jit(solution)/shard_map/cocluster/pallas_call | solution.py:656
  187.3 1.9 copy.26
  189.2 1.5 copy.27
  (11 shorter events, 0.1 us)

commit v6 on v5

--- a/solution.py
+++ b/solution.py
@@ -15,7 +15,7 @@
 UT = 64
 IT = 64
 ITERS = 2
-UNROLL = 64
+UNROLL = 72
 LOADS = 4
 NCH = 2
 SIZE = 16 // NCH

time: 191 us -> 191 us (level)
  no operation moved by 1% of the time
where the time goes in v6:
time: 191 us; the launch traced here: 190 us
  Pallas kernels  182 us (95%)
  local copies, waits for them, and re-layouts  3.36 us (2%)
  other arithmetic  3.28 us (2%)
    pallas_call x1, Pallas kernels, whole_call(): pl.pallas_call(functools.partial(whole_kernel, user_total, item_total), o...  182 us

profile of v6, /device:TPU:1, one launch (start us, length us, event | category | flops | bytes accessed | tf_op | source)
XLA Modules:
  0.0 190.4 jit_solution(7170346387116636867)
XLA Ops:
  1.3 0.8 broadcast_add_fusion.1
  2.1 0.1 convert_reduce_fusion.1
  2.2 0.1 select_reduce_fusion.2
  2.4 0.6 pad_add_fusion.1.last_s
  3.0 0.1 select_reduce_fusion.1
  3.1 0.4 convert_reduce_fusion
  3.5 0.4 select_reduce_fusion
  3.9 0.1 compare_convert_fusion
  4.0 0.6 pad_add_fusion.order_s
  4.7 182.4 %cocluster.1 = (f32[64,2048]{1,0:T(8,128)}, f32[64,256]{1,0:T(8,128)}) custom-call(s32[2,3,576]{2,1,0:T(4,128)} %pad_add_fusion.order_s, s32[2,2,64]{2,1,0:T(2,128)} %pad_add_fusion.1.last_s, bf16[64,256]{1,0:T(8,128)(2,1)} %start_ref.1, s32[16,128]{1,0:T(8,128)} %bitcast.32, s32[2,128]{1,0:T(2,128)} %bitcast.37, bf16[512,128,128]{2,1,0:T(8,128)(2,1)} %bitcast.30), custom_call_target="tpu_custom_call" | custom-call | tf_op jit(solution)/shard_map/cocluster/pallas_call | solution.py:656
  187.0 1.9 copy.26
  188.9 1.5 copy.27
  (11 shorter events, 0.1 us)
